TPU v7x, 128 devices: a whole 4x4x4 slice. The times are simulated.
128 devices in a mesh: ctx: 16 (over z_lo, x, core), head: 8 (over y, z_hi).
Axes of the slice: x: 4, y: 4, z: 4 (z_hi: 2, z_lo: 2; z = z_hi * 2 + z_lo), core: 2. Of those that a mesh axis runs over, the one named last changes fastest.
Arguments:
- node_rows: bfloat16 [8192, 4096], P('ctx', 'head')
- node_target: int32 [8192], P('ctx'), may hold values from 0 to 8191, as said below
- node_position: int32 [8192], P('ctx'), may hold values from 0 to 8191
- block_mask: int32 [64, 64], P('ctx'), may hold values from 0 to 1, as said below
- w_query: bfloat16 [4096, 4096], P(None, 'head'), may hold values from -0.09375 to 0.09375
- w_key: bfloat16 [4096, 1024], P(None, 'head'), may hold values from -0.09375 to 0.09375
- w_value: bfloat16 [4096, 1024], P(None, 'head'), may hold values from -0.09375 to 0.09375
- w_out: bfloat16 [4096, 4096], P('head'), may hold values from -0.09375 to 0.09375
Outputs:
- scored: bfloat16 [8192, 4096], P(('ctx', 'head'))
Inputs may be any that keep to these rules, and one draw needn't show every extreme that they name: node_target is a permutation of the 8192 tree positions; the rows that one generator device holds send at most 64 rows to the 512 positions of one owner, and exactly 64 to some owner. block_mask[qb, kb] is 1 exactly when block kb lies strictly above block qb on its path to the root of a tree of blocks whose root is block 0; entries with kb >= qb are 0.
All inputs are finite; a program needn't handle non-finite values.
Results may differ from a plain program's by a relative error of at most 0.025.
The roundings to bfloat16 on the way count: a program that leaves them out, or rounds other values in their place, can miss the bound.
Values may be sent and summed in bfloat16 or wider, within the bound.
A program may use at most 64 MiB of HBM per device.

v0:
```python
import math

import jax
import jax.numpy as jnp
from jax import lax
from jax.sharding import PartitionSpec as P

HD = 128
BLOCK = 128


ROPE_THETA = 500000.0
NEG_LARGE = -1e30


def rotate(tensor, positions, head_size):
    half_size = head_size // 2
    inverse = jnp.exp(
        jnp.arange(half_size, dtype=jnp.float32) * (-2.0 * math.log(ROPE_THETA) / head_size)
    )
    angles = positions.astype(jnp.float32)[:, None] * inverse[None, :]
    cosine = jnp.cos(angles)[:, None, :]
    sine = jnp.sin(angles)[:, None, :]
    first_half = tensor[..., :half_size]
    second_half = tensor[..., half_size:]
    return jnp.concatenate(
        [first_half * cosine - second_half * sine, second_half * cosine + first_half * sine],
        axis=-1,
    )


def on_device(node_rows, node_target, node_position, block_mask, w_query, w_key, w_value, w_out):
    local_rows = node_rows.shape[0]
    row_offset = lax.axis_index("ctx") * local_rows
    all_rows, all_targets = (
        lax.all_gather(node_rows, "ctx", axis=0, tiled=True),
        lax.all_gather(node_target, "ctx", axis=0, tiled=True),
    )
    places = all_targets - row_offset
    places = jnp.where((places >= 0) & (places < local_rows), places, local_rows)
    routed = jnp.zeros_like(node_rows).at[places].set(all_rows, mode="drop")
    pieces_in = lax.all_gather(routed, "head", axis=1, tiled=True)
    query_proj, key_proj, value_proj = tuple(
        (
            jnp.dot(pieces_in, weight, preferred_element_type=jnp.float32)
            for weight in (w_query, w_key, w_value)
        )
    )
    head_size = HD
    query_heads = w_query.shape[1] // head_size
    kv_local = w_key.shape[1] // head_size
    groups = query_heads // kv_local
    queries = rotate(
        query_proj.reshape(local_rows, query_heads, head_size), node_position, head_size
    ).astype(jnp.bfloat16)
    queries = jnp.transpose(queries.reshape(local_rows, kv_local, groups, head_size), (1, 2, 0, 3))
    keys_local = (
        rotate(key_proj.reshape(local_rows, kv_local, head_size), node_position, head_size)
        .astype(jnp.bfloat16)
        .reshape(local_rows, kv_local * head_size)
    )
    values_local = value_proj.astype(jnp.bfloat16)
    query_index = row_offset + jnp.arange(local_rows, dtype=jnp.int32)
    query_block = query_index // BLOCK
    mask_float = block_mask.astype(jnp.float32)
    block_count = block_mask.shape[1]
    inverse_root = 1.0 / math.sqrt(head_size)

    def update(state, key_tile, value_tile, key_index):
        key_block = key_index // BLOCK
        selector = (jnp.arange(block_count, dtype=jnp.int32)[:, None] == key_block[None, :]).astype(
            jnp.float32
        )
        allowed_rows = jnp.repeat(jnp.dot(mask_float, selector), BLOCK, axis=0)
        earlier = (key_block[None, :] < query_block[:, None]) & (allowed_rows > 0.5)
        diagonal = (key_block[None, :] == query_block[:, None]) & (
            key_index[None, :] <= query_index[:, None]
        )
        allowed = earlier | diagonal
        running_max, denominators, weighted = state
        scores = (
            jnp.einsum("kgqd,nkd->kgqn", queries, key_tile, preferred_element_type=jnp.float32)
            * inverse_root
        )
        masked = jnp.where(allowed[None, None], scores, NEG_LARGE)
        new_max = jnp.maximum(running_max, jnp.max(masked, axis=-1))
        weights = jnp.where(allowed[None, None], jnp.exp(scores - new_max[..., None]), 0.0)
        factor = jnp.exp(running_max - new_max)
        denominators = denominators * factor + jnp.sum(weights, axis=-1)
        weighted = weighted * factor[..., None] + jnp.einsum(
            "kgqn,nkd->kgqd",
            weights.astype(jnp.bfloat16),
            value_tile,
            preferred_element_type=jnp.float32,
        )
        return (new_max, denominators, weighted)

    initial = (
        jnp.full((kv_local, groups, local_rows), NEG_LARGE, jnp.float32),
        jnp.zeros((kv_local, groups, local_rows), jnp.float32),
        jnp.zeros((kv_local, groups, local_rows, head_size), jnp.float32),
    )
    key_piece = lax.all_gather(keys_local, "ctx", axis=0, tiled=True)
    value_piece = lax.all_gather(values_local, "ctx", axis=0, tiled=True)
    length = key_piece.shape[0]
    tile_width = math.gcd(length, 512)

    def one_tile(tile_number, state):
        begin = tile_number * tile_width
        key_tile = lax.dynamic_slice_in_dim(key_piece, begin, tile_width, 0).reshape(
            tile_width, kv_local, head_size
        )
        value_tile = lax.dynamic_slice_in_dim(value_piece, begin, tile_width, 0).reshape(
            tile_width, kv_local, head_size
        )
        key_index = begin + jnp.arange(tile_width, dtype=jnp.int32)
        return update(state, key_tile, value_tile, key_index)

    running_max, denominators, weighted = lax.fori_loop(0, length // tile_width, one_tile, initial)
    attended = (weighted / denominators[..., None]).astype(jnp.bfloat16)
    attended = jnp.transpose(attended, (2, 0, 1, 3)).reshape(local_rows, query_heads * head_size)
    return lax.psum_scatter(
        jnp.dot(attended, w_out, preferred_element_type=jnp.float32).astype(jnp.bfloat16),
        "head",
        scatter_dimension=0,
        tiled=True,
    )


def solution(mesh):
    placed = (
        P("ctx", "head"),
        P("ctx"),
        P("ctx"),
        P("ctx", None),
        P(None, "head"),
        P(None, "head"),
        P(None, "head"),
        P("head", None),
    )
    return jax.shard_map(
        on_device, mesh=mesh, in_specs=placed, out_specs=P(("ctx", "head"), None), check_vma=False
    )
```

profile of v0, /device:TPU:34, one launch (start us, length us, event | category | flops | bytes accessed | tf_op | source)
XLA Modules:
  0.0 529.9 jit_solution(13107175953731601208)
XLA Ops:
  7.3 16.9 %all-gather = s32[16,1,512]{2,1,0:T(1,128)S(1)} all-gather(s32[1,1,512]{2,1,0:T(1,128)} %bitcast.119), channel_id=1, replica_groups=mesh['ctx'=16,'head'=8] {'ctx'}, dimensions={0}, use_global_device_ids=true | all-gather | bytes 34816 | tf_op jit(solution)/shard_map/all_gather | solution.py:37
  24.2 39.0 %all-gather.6.cloned.1.call-done = bf16[8192,512]{1,0:T(8,128)(2,1)} async-done(((bf16[512,512]{1,0:T(8,128)(2,1)}), bf16[8192,512]{1,0:T(8,128)(2,1)}) %all-gather.6.cloned.1.call-update) | async-done | bytes 8388624 | tf_op jit(solution)/shard_map/all_gather | solution.py:36
  63.2 36.6 %scatter_custom_fusion = bf16[512,512]{1,0:T(8,128)(2,1)} fusion(s32[8192]{0:T(1024)S(1)} %compare_select_fusion, bf16[8192,512]{1,0:T(8,128)(2,1)} %all-gather.6.cloned.1.call-done, bf16[]{:T(256)} %constant.148.clone.1), kind=kCustom, calls=%fused_computation.65 | custom fusion | bytes 524800 | tf_op jit(solution)/shard_map/scatter | solution.py:41
  100.5 77.7 %all-gather.8.cloned.1.call-done = bf16[512,4096]{1,0:T(8,128)(2,1)} async-done(((bf16[512,512]{1,0:T(8,128)(2,1)}), bf16[512,4096]{1,0:T(8,128)(2,1)}) %all-gather.8.cloned.1.call-update) | async-done | bytes 4194320 | tf_op jit(solution)/shard_map/all_gather | solution.py:42
  183.2 4.1 convolution_convert_fusion.1
  189.4 5.9 %fusion.53 = f32[512,512]{0,1:T(8,128)S(1)} fusion(bf16[512,4096]{1,0:T(8,128)(2,1)} %all-gather.8.cloned.1.call-done, bf16[4096,512]{1,0:T(8,128)(2,1)} %param.14), kind=kOutput, calls=%fused_computation.84 | convolution fusion | flops 2147483648 | bytes 9437184 | tf_op jit(solution)/shard_map/dot_general | solution.py:45
  199.5 16.2 %all-gather.10.cloned.1.call-done = bf16[8192,128]{0,1:T(8,128)(2,1)} async-done(((bf16[512,128]{0,1:T(8,128)(2,1)}), bf16[8192,128]{0,1:T(8,128)(2,1)}) %all-gather.10.cloned.1.call-update) | async-done | bytes 2097168 | tf_op jit(solution)/shard_map/all_gather | solution.py:103
  215.7 35.6 %all-gather.12.cloned.1.call-done = bf16[8192,128]{1,0:T(8,128)(2,1)} async-done(((bf16[512,128]{1,0:T(8,128)(2,1)}), bf16[8192,128]{1,0:T(8,128)(2,1)}) %all-gather.12.cloned.1.call-update) | async-done | bytes 2097168 | tf_op jit(solution)/shard_map/all_gather | solution.py:104
  251.3 178.4 %while.22 = (s32[]{:T(128)}, f32[1,4,512]{2,1,0:T(4,128)S(1)}, f32[1,4,512]{2,1,0:T(4,128)S(1)}, f32[1,4,512,128]{3,2,1,0:T(8,128)}, bf16[4,64]{1,0:T(4,128)(2,1...) while((s32[]{:T(128)}, f32[1,4,512]{2,1,0:T(4,128)S(1)}, ...), condition=%wide.region_4.5_spmd.clone.clone.clone, body=%wide.region_1.4_spmd.clone.clone.clone.sunk | while | flops 551090176 | bytes 42363672 | solution.py:119
  268.7 3.8 fusion.80
  279.9 3.8 fusion.80
  291.0 3.8 fusion.80
  302.2 3.8 fusion.80
  313.3 3.8 fusion.80
  324.5 3.8 fusion.80
  335.6 3.8 fusion.80
  346.8 3.8 fusion.80
  357.9 3.8 fusion.80
  369.1 3.8 fusion.80
  391.4 3.8 fusion.80
  402.5 3.8 fusion.80
  424.8 3.8 fusion.80
  431.4 6.5 %convolution_convert_fusion = bf16[512,4096]{1,0:T(8,128)(2,1)} fusion(bf16[512,512]{0,1:T(8,128)(2,1)S(1)} %bitcast.114, bf16[512,4096]{1,0:T(8,128)(2,1)} %param.17), kind=kOutput, calls=%fused_computation.54 | convolution fusion | flops 2149580800 | bytes 8912896 | tf_op jit(solution)/shard_map/dot_general | solution.py:123
  438.0 85.4 %reduce-scatter.2.cloned.1.call-done = bf16[64,4096]{1,0:T(8,128)(2,1)} async-done(((bf16[512,4096]{1,0:T(8,128)(2,1)}), bf16[64,4096]{1,0:T(8,128)(2,1)}) %reduce-scatter.2.cloned.1.call-update) | async-done | bytes 524304 | tf_op jit(solution)/shard_map/reduce_scatter | solution.py:122
  (310 shorter events, 141.5 us)
Async XLA Ops:
  6.5 171.7 %copy-start = (bf16[4096,128]{1,0:T(8,128)(2,1)S(1)}, bf16[4096,128]{1,0:T(8,128)(2,1)}, u32[]{:S(2)}) copy-start(bf16[4096,128]{1,0:T(8,128)(2,1)} %param.15) | copy-start | bytes 3145732
  6.5 56.6 %all-gather.6.cloned.1.call-start = ((), (), s32[]{:S(2)}) async-start(), calls=%async_computation.1 | async-start | bytes 8912896 | tf_op jit(solution)/shard_map/all_gather | solution.py:36
  7.3 170.9 %all-gather.8.cloned.1.call-start = ((), (), s32[]{:S(2)}) async-start(), calls=%async_computation.2 | async-start | bytes 4718592 | tf_op jit(solution)/shard_map/all_gather | solution.py:42
  99.8 116.0 %all-gather.10.cloned.1.call-start = ((), (), s32[]{:S(2)}) async-start(), calls=%async_computation.3 | async-start | bytes 2228224 | tf_op jit(solution)/shard_map/all_gather | solution.py:103
  100.5 82.7 %copy-start.5 = (bf16[4096,128]{1,0:T(8,128)(2,1)S(1)}, bf16[4096,128]{1,0:T(8,128)(2,1)}, u32[]{:S(2)}) copy-start(bf16[4096,128]{1,0:T(8,128)(2,1)} %param.16) | copy-start | bytes 3145732
  181.9 5.7 %copy-start.4 = (s32[4,64]{1,0:T(4,128)S(1)}, s32[4,64]{1,0:T(4,128)}, u32[]{:S(2)}) copy-start(s32[4,64]{1,0:T(4,128)} %param.13) | copy-start | bytes 3076
  183.2 68.2 %all-gather.12.cloned.1.call-start = ((), (), s32[]{:S(2)}) async-start(), calls=%async_computation.4 | async-start | bytes 2228224 | tf_op jit(solution)/shard_map/all_gather | solution.py:104
  187.3 336.1 %reduce-scatter.2.cloned.1.call-start = ((), (), s32[]{:S(2)}) async-start(), calls=%async_computation.5 | async-start | bytes 4718592 | tf_op jit(solution)/shard_map/reduce_scatter | solution.py:122
  251.3 6.2 %copy-start.2 = (f32[1,4,512,128]{3,2,1,0:T(8,128)S(1)}, f32[1,4,512,128]{3,2,1,0:T(8,128)}, u32[]{:S(2)}) copy-start(f32[1,4,512,128]{3,2,1,0:T(8,128)} %get-tuple-element.485) | copy-start | bytes 3145732 | tf_op jit(solution)/shard_map/while
  262.5 6.2 %copy-start.2 = (f32[1,4,512,128]{3,2,1,0:T(8,128)S(1)}, f32[1,4,512,128]{3,2,1,0:T(8,128)}, u32[]{:S(2)}) copy-start(f32[1,4,512,128]{3,2,1,0:T(8,128)} %get-tuple-element.485) | copy-start | bytes 3145732 | tf_op jit(solution)/shard_map/while
  273.6 6.2 %copy-start.2 = (f32[1,4,512,128]{3,2,1,0:T(8,128)S(1)}, f32[1,4,512,128]{3,2,1,0:T(8,128)}, u32[]{:S(2)}) copy-start(f32[1,4,512,128]{3,2,1,0:T(8,128)} %get-tuple-element.485) | copy-start | bytes 3145732 | tf_op jit(solution)/shard_map/while
  284.8 6.2 %copy-start.2 = (f32[1,4,512,128]{3,2,1,0:T(8,128)S(1)}, f32[1,4,512,128]{3,2,1,0:T(8,128)}, u32[]{:S(2)}) copy-start(f32[1,4,512,128]{3,2,1,0:T(8,128)} %get-tuple-element.485) | copy-start | bytes 3145732 | tf_op jit(solution)/shard_map/while
  295.9 6.2 %copy-start.2 = (f32[1,4,512,128]{3,2,1,0:T(8,128)S(1)}, f32[1,4,512,128]{3,2,1,0:T(8,128)}, u32[]{:S(2)}) copy-start(f32[1,4,512,128]{3,2,1,0:T(8,128)} %get-tuple-element.485) | copy-start | bytes 3145732 | tf_op jit(solution)/shard_map/while
  307.1 6.2 %copy-start.2 = (f32[1,4,512,128]{3,2,1,0:T(8,128)S(1)}, f32[1,4,512,128]{3,2,1,0:T(8,128)}, u32[]{:S(2)}) copy-start(f32[1,4,512,128]{3,2,1,0:T(8,128)} %get-tuple-element.485) | copy-start | bytes 3145732 | tf_op jit(solution)/shard_map/while
  318.2 6.2 %copy-start.2 = (f32[1,4,512,128]{3,2,1,0:T(8,128)S(1)}, f32[1,4,512,128]{3,2,1,0:T(8,128)}, u32[]{:S(2)}) copy-start(f32[1,4,512,128]{3,2,1,0:T(8,128)} %get-tuple-element.485) | copy-start | bytes 3145732 | tf_op jit(solution)/shard_map/while
  329.4 6.2 %copy-start.2 = (f32[1,4,512,128]{3,2,1,0:T(8,128)S(1)}, f32[1,4,512,128]{3,2,1,0:T(8,128)}, u32[]{:S(2)}) copy-start(f32[1,4,512,128]{3,2,1,0:T(8,128)} %get-tuple-element.485) | copy-start | bytes 3145732 | tf_op jit(solution)/shard_map/while
  340.5 6.2 %copy-start.2 = (f32[1,4,512,128]{3,2,1,0:T(8,128)S(1)}, f32[1,4,512,128]{3,2,1,0:T(8,128)}, u32[]{:S(2)}) copy-start(f32[1,4,512,128]{3,2,1,0:T(8,128)} %get-tuple-element.485) | copy-start | bytes 3145732 | tf_op jit(solution)/shard_map/while
  351.7 6.2 %copy-start.2 = (f32[1,4,512,128]{3,2,1,0:T(8,128)S(1)}, f32[1,4,512,128]{3,2,1,0:T(8,128)}, u32[]{:S(2)}) copy-start(f32[1,4,512,128]{3,2,1,0:T(8,128)} %get-tuple-element.485) | copy-start | bytes 3145732 | tf_op jit(solution)/shard_map/while
  362.8 6.2 %copy-start.2 = (f32[1,4,512,128]{3,2,1,0:T(8,128)S(1)}, f32[1,4,512,128]{3,2,1,0:T(8,128)}, u32[]{:S(2)}) copy-start(f32[1,4,512,128]{3,2,1,0:T(8,128)} %get-tuple-element.485) | copy-start | bytes 3145732 | tf_op jit(solution)/shard_map/while
  374.0 6.2 %copy-start.2 = (f32[1,4,512,128]{3,2,1,0:T(8,128)S(1)}, f32[1,4,512,128]{3,2,1,0:T(8,128)}, u32[]{:S(2)}) copy-start(f32[1,4,512,128]{3,2,1,0:T(8,128)} %get-tuple-element.485) | copy-start | bytes 3145732 | tf_op jit(solution)/shard_map/while
  385.1 6.2 %copy-start.2 = (f32[1,4,512,128]{3,2,1,0:T(8,128)S(1)}, f32[1,4,512,128]{3,2,1,0:T(8,128)}, u32[]{:S(2)}) copy-start(f32[1,4,512,128]{3,2,1,0:T(8,128)} %get-tuple-element.485) | copy-start | bytes 3145732 | tf_op jit(solution)/shard_map/while
  396.3 6.2 %copy-start.2 = (f32[1,4,512,128]{3,2,1,0:T(8,128)S(1)}, f32[1,4,512,128]{3,2,1,0:T(8,128)}, u32[]{:S(2)}) copy-start(f32[1,4,512,128]{3,2,1,0:T(8,128)} %get-tuple-element.485) | copy-start | bytes 3145732 | tf_op jit(solution)/shard_map/while
  407.4 6.2 %copy-start.2 = (f32[1,4,512,128]{3,2,1,0:T(8,128)S(1)}, f32[1,4,512,128]{3,2,1,0:T(8,128)}, u32[]{:S(2)}) copy-start(f32[1,4,512,128]{3,2,1,0:T(8,128)} %get-tuple-element.485) | copy-start | bytes 3145732 | tf_op jit(solution)/shard_map/while
  418.6 6.2 %copy-start.2 = (f32[1,4,512,128]{3,2,1,0:T(8,128)S(1)}, f32[1,4,512,128]{3,2,1,0:T(8,128)}, u32[]{:S(2)}) copy-start(f32[1,4,512,128]{3,2,1,0:T(8,128)} %get-tuple-element.485) | copy-start | bytes 3145732 | tf_op jit(solution)/shard_map/while
  (32 other events, 78.9 us)
Sparse Core Ops, SparseCore 0:
  9.1 54.0 all-gather.5
  99.9 78.2 all-gather.7
  183.3 32.3 all-gather.9
  217.3 34.0 all-gather.11
  438.1 85.2 reduce-scatter.1
where the time goes:
time: 532 us; the launch traced here: 530 us
  waiting for transfers between devices  255 us (48%)
  matrix products  144 us (27%)
  local copies, waits for them, and re-layouts  71 us (13%)
  other arithmetic  28.2 us (5%)
  blocking collectives  16.9 us (3%)
  between operations  13.3 us (2%)
    reduce_scatter x1, waiting for transfers between devices, on_device(): lax.psum_scatter(jnp.dot(attended, w_out, preferred_element_type=jnp.floa...  85.4 us
    all_gather x1, waiting for transfers between devices, on_device(): pieces_in = lax.all_gather(routed, 'head', axis=1, tiled=True)  77.7 us
    dot_general x16, matrix products, update(): jnp.einsum('kgqn,nkd->kgqd', weights.astype(jnp.bfloat16), value_tile, pr...  61.3 us
    dot_general x16, matrix products, update(): jnp.einsum('kgqd,nkd->kgqn', queries, key_tile, preferred_element_type=jn...  60.2 us
    all_gather x1, waiting for transfers between devices, on_device(): lax.all_gather(node_rows, 'ctx', axis=0, tiled=True)  39 us
    scatter x1, local copies, waits for them, and re-layouts, on_device(): routed = jnp.zeros_like(node_rows).at[places].set(all_rows, mode='drop')  36.6 us
    all_gather x1, waiting for transfers between devices, on_device(): value_piece = lax.all_gather(values_local, 'ctx', axis=0, tiled=True)  35.6 us
    broadcast_in_dim x16, local copies, waits for them, and re-layouts, update(): allowed_rows = jnp.repeat(jnp.dot(mask_float, selector), BLOCK, axis=0)  25.6 us
  transfers between devices with their start and end apart: 5, of which 5 were waited for; matrix products, arithmetic and copies ran while one was open for 3% of the time, Pallas kernels for 0%

commit v1 on v0

v1 whole, which is shorter than its diff:
```python
import functools
import math

import jax
import jax.numpy as jnp
from jax import lax
from jax.experimental import pallas as pl
from jax.experimental.pallas import tpu as pltpu
from jax.sharding import PartitionSpec as P

HD = 128
BLOCK = 128
ROPE_THETA = 500000.0
NEG_LARGE = -1e30
MIB = 1024 * 1024


def rotary_tables(positions, head_size):
    half_size = head_size // 2
    inverse = jnp.exp(
        jnp.arange(half_size, dtype=jnp.float32) * (-2.0 * math.log(ROPE_THETA) / head_size)
    )
    angles = positions.astype(jnp.float32)[:, None] * inverse[None, :]
    cosine = jnp.cos(angles)
    sine = jnp.sin(angles)
    return jnp.concatenate([cosine, cosine], axis=-1), jnp.concatenate([-sine, sine], axis=-1)


def attend_kernel(mask_ref, q_ref, kv_ref, out_ref, list_ref, acc_ref):
    ctx = lax.axis_index("ctx")
    local_blocks = q_ref.shape[0] // BLOCK
    heads = q_ref.shape[1] // HD
    block_count = mask_ref.shape[1]
    width = heads * BLOCK
    scale = 1.0 / math.sqrt(HD)

    for b in range(local_blocks):
        qb = ctx * local_blocks + b

        def build(kb, n):
            list_ref[n] = kb
            return n + jnp.where(kb < qb, mask_ref[b, kb], 0)

        count = lax.fori_loop(0, block_count, build, 0, unroll=8)
        list_ref[count] = 0
        rows = pl.ds(b * BLOCK, BLOCK)
        queries = jnp.concatenate(
            [q_ref[rows, h * HD : (h + 1) * HD] for h in range(heads)], axis=0
        )

        def scores_of(kb):
            keys = kv_ref[pl.ds(pl.multiple_of(kb * BLOCK, BLOCK), BLOCK), 0:HD]
            return (
                lax.dot_general(
                    keys, queries, (((1,), (1,)), ((), ())), preferred_element_type=jnp.float32
                )
                * scale
            )

        def mix(kb, weights):
            values = kv_ref[pl.ds(pl.multiple_of(kb * BLOCK, BLOCK), BLOCK), HD : 2 * HD]
            return lax.dot_general(
                values,
                weights.astype(jnp.bfloat16),
                (((0,), (0,)), ((), ())),
                preferred_element_type=jnp.float32,
            )

        key_at = lax.broadcasted_iota(jnp.int32, (BLOCK, width), 0)
        query_at = lax.broadcasted_iota(jnp.int32, (BLOCK, width), 1) % BLOCK
        scores = jnp.where(key_at <= query_at, scores_of(qb), NEG_LARGE)
        highest = jnp.max(scores, axis=0, keepdims=True)
        weights = jnp.exp(scores - highest)
        total = jnp.sum(weights, axis=0, keepdims=True)
        acc_ref[...] = mix(qb, weights)

        def step(i, state):
            highest, total = state
            first = list_ref[2 * i]
            second = list_ref[2 * i + 1]
            has_second = 2 * i + 1 < count
            second = jnp.where(has_second, second, 0)
            drop = jnp.where(has_second, 0.0, NEG_LARGE).astype(jnp.float32)
            scores0 = scores_of(first)
            scores1 = scores_of(second) + drop
            new_highest = jnp.maximum(
                highest,
                jnp.maximum(
                    jnp.max(scores0, axis=0, keepdims=True), jnp.max(scores1, axis=0, keepdims=True)
                ),
            )
            factor = jnp.exp(highest - new_highest)
            weights0 = jnp.exp(scores0 - new_highest)
            weights1 = jnp.exp(scores1 - new_highest)
            total = (
                total * factor
                + jnp.sum(weights0, axis=0, keepdims=True)
                + jnp.sum(weights1, axis=0, keepdims=True)
            )
            acc_ref[...] = acc_ref[...] * factor + mix(first, weights0) + mix(second, weights1)
            return new_highest, total

        highest, total = lax.fori_loop(0, (count + 1) // 2, step, (highest, total))
        attended = acc_ref[...] / total
        for h in range(heads):
            out_ref[rows, h * HD : (h + 1) * HD] = attended[
                :, h * BLOCK : (h + 1) * BLOCK
            ].T.astype(jnp.bfloat16)


def attend(block_mask, queries, kv):
    return pl.pallas_call(
        attend_kernel,
        out_shape=jax.ShapeDtypeStruct(queries.shape, jnp.bfloat16),
        in_specs=[
            pl.BlockSpec(memory_space=pltpu.SMEM),
            pl.BlockSpec(memory_space=pltpu.VMEM),
            pl.BlockSpec(memory_space=pltpu.VMEM),
        ],
        out_specs=pl.BlockSpec(memory_space=pltpu.VMEM),
        scratch_shapes=[
            pltpu.SMEM((128,), jnp.int32),
            pltpu.VMEM((HD, queries.shape[1]), jnp.float32),
        ],
        compiler_params=pltpu.CompilerParams(vmem_limit_bytes=32 * MIB),
        name="attend",
    )(block_mask, queries, kv)


def on_device(node_rows, node_target, node_position, block_mask, w_query, w_key, w_value, w_out):
    local_rows = node_rows.shape[0]
    row_offset = lax.axis_index("ctx") * local_rows
    all_rows, all_targets = (
        lax.all_gather(node_rows, "ctx", axis=0, tiled=True),
        lax.all_gather(node_target, "ctx", axis=0, tiled=True),
    )
    places = all_targets - row_offset
    places = jnp.where((places >= 0) & (places < local_rows), places, local_rows)
    routed = jnp.zeros_like(node_rows).at[places].set(all_rows, mode="drop")
    pieces_in = lax.all_gather(routed, "head", axis=1, tiled=True)
    query_proj, key_proj, value_proj = tuple(
        (
            jnp.dot(pieces_in, weight, preferred_element_type=jnp.float32)
            for weight in (w_query, w_key, w_value)
        )
    )
    cosine, sine = rotary_tables(node_position, HD)

    def rotate(tensor):
        heads = tensor.reshape(local_rows, -1, HD)
        turned = jnp.roll(heads, HD // 2, axis=-1)
        return (
            (heads * cosine[:, None, :] + turned * sine[:, None, :])
            .astype(jnp.bfloat16)
            .reshape(tensor.shape)
        )

    queries = rotate(query_proj)
    kv_local = jnp.concatenate([rotate(key_proj), value_proj.astype(jnp.bfloat16)], axis=1)
    kv = lax.all_gather(kv_local, "ctx", axis=0, tiled=True)
    attended = attend(block_mask, queries, kv)
    return lax.psum_scatter(
        jnp.dot(attended, w_out, preferred_element_type=jnp.float32).astype(jnp.bfloat16),
        "head",
        scatter_dimension=0,
        tiled=True,
    )


def solution(mesh):
    placed = (
        P("ctx", "head"),
        P("ctx"),
        P("ctx"),
        P("ctx", None),
        P(None, "head"),
        P(None, "head"),
        P(None, "head"),
        P("head", None),
    )
    return jax.shard_map(
        on_device, mesh=mesh, in_specs=placed, out_specs=P(("ctx", "head"), None), check_vma=False
    )
```

time: 532 us -> 331 us (0.62)
  matrix products: 144 us -> 15 us
  waiting for transfers between devices: 255 us -> 225 us
  local copies, waits for them, and re-layouts: 71 us -> 44.3 us
  other arithmetic: 28.2 us -> 5.77 us
  Pallas kernels: 0 us -> 8.42 us
    dot_general x48 -> x0, matrix products: 124 us -> none  [the longest x16 61.3 us: update(): jnp.einsum('kgqn,nkd->kgqd', weights.astype(jnp.bfloat16), value_tile, pr...]
    all_gather x2 -> x1, waiting for transfers between devices: 51.9 us -> 22.5 us  [on_device(): kv = lax.all_gather(kv_local, 'ctx', axis=0, tiled=True)]
    broadcast_in_dim x16 -> x0, local copies, waits for them, and re-layouts: 25.6 us -> none  [update(): allowed_rows = jnp.repeat(jnp.dot(mask_float, selector), BLOCK, axis=0)]
    reduce_sum x16 -> x0, other arithmetic: 14.7 us -> none  [update(): denominators = denominators * factor + jnp.sum(weights, axis=-1)]
    pallas_call x0 -> x1, Pallas kernels: none -> 8.42 us  [attend(): pl.pallas_call(attend_kernel, out_shape=jax.ShapeDtypeStruct(queries.shap...]
    or x16 -> x0, other arithmetic: 7.21 us -> none  [update(): allowed = earlier | diagonal]
  transfers between devices with their start and end apart: 5 -> 4, of which waited for: 5 -> 4; matrix products, arithmetic and copies ran while one was open for 3% -> 5% of each run, Pallas kernels for 0% -> 0%
where the time goes in v1:
time: 331 us; the launch traced here: 329 us
  waiting for transfers between devices  225 us (68%)
  local copies, waits for them, and re-layouts  44.3 us (13%)
  blocking collectives  16.9 us (5%)
  matrix products  15 us (5%)
  between operations  13.2 us (4%)
  Pallas kernels  8.42 us (3%)
  other arithmetic  5.77 us (2%)
    reduce_scatter x1, waiting for transfers between devices, on_device(): lax.psum_scatter(jnp.dot(attended, w_out, preferred_element_type=jnp.floa...  86.4 us
    all_gather x1, waiting for transfers between devices, on_device(): pieces_in = lax.all_gather(routed, 'head', axis=1, tiled=True)  76.7 us
    all_gather x1, waiting for transfers between devices, on_device(): lax.all_gather(node_rows, 'ctx', axis=0, tiled=True)  39 us
    scatter x1, local copies, waits for them, and re-layouts, on_device(): routed = jnp.zeros_like(node_rows).at[places].set(all_rows, mode='drop')  36.6 us
    all_gather x1, waiting for transfers between devices, on_device(): kv = lax.all_gather(kv_local, 'ctx', axis=0, tiled=True)  22.5 us
    all_gather x1, blocking collectives, on_device(): lax.all_gather(node_target, 'ctx', axis=0, tiled=True)  16.9 us
    dot_general x3, matrix products, on_device(): jnp.dot(pieces_in, weight, preferred_element_type=jnp.float32)  10.7 us
    pallas_call x1, Pallas kernels, attend(): pl.pallas_call(attend_kernel, out_shape=jax.ShapeDtypeStruct(queries.shap...  8.42 us
  transfers between devices with their start and end apart: 4, of which 4 were waited for; matrix products, arithmetic and copies ran while one was open for 5% of the time, Pallas kernels for 0%

profile of v1, /device:TPU:34, one launch (start us, length us, event | category | flops | bytes accessed | tf_op | source)
XLA Modules:
  0.0 329.0 jit_solution(17961974529217330700)
XLA Ops:
  6.5 0.7 all-gather.5.cloned.1.call-update
  7.3 16.9 %all-gather = s32[16,1,512]{2,1,0:T(1,128)S(1)} all-gather(s32[1,1,512]{2,1,0:T(1,128)} %bitcast.34), channel_id=1, replica_groups=mesh['ctx'=16,'head'=8] {'ctx'}, dimensions={0}, use_global_device_ids=true | all-gather | bytes 34816 | tf_op jit(solution)/shard_map/all_gather | solution.py:135
  24.2 39.0 %all-gather.5.cloned.1.call-done = bf16[8192,512]{1,0:T(8,128)(2,1)} async-done(((bf16[512,512]{1,0:T(8,128)(2,1)}), bf16[8192,512]{1,0:T(8,128)(2,1)}) %all-gather.5.cloned.1.call-update) | async-done | bytes 8388624 | tf_op jit(solution)/shard_map/all_gather | solution.py:134
  63.2 36.6 %scatter_custom_fusion = bf16[512,512]{1,0:T(8,128)(2,1)} fusion(s32[8192]{0:T(1024)S(1)} %compare_select_fusion, bf16[8192,512]{1,0:T(8,128)(2,1)} %all-gather.5.cloned.1.call-done, bf16[]{:T(256)} %constant.6.clone.1), kind=kCustom, calls=%fused_computation.17 | custom fusion | bytes 524800 | tf_op jit(solution)/shard_map/scatter | solution.py:139
  99.8 0.7 convert_element_type.17
  100.5 1.0 fusion.5
  101.5 76.7 %all-gather.7.cloned.1.call-done = bf16[512,4096]{1,0:T(8,128)(2,1)} async-done(((bf16[512,512]{1,0:T(8,128)(2,1)}), bf16[512,4096]{1,0:T(8,128)(2,1)}) %all-gather.7.cloned.1.call-update) | async-done | bytes 4194320 | tf_op jit(solution)/shard_map/all_gather | solution.py:140
  178.2 3.6 %fusion.8 = f32[512,128]{1,0:T(8,128)S(1)} fusion(bf16[512,4096]{1,0:T(8,128)(2,1)} %all-gather.7.cloned.1.call-done, bf16[4096,128]{1,0:T(8,128)(2,1)S(1)} %copy-done), kind=kOutput, calls=%fused_computation.25 | convolution fusion | flops 536870912 | bytes 5505024 | tf_op jit(solution)/shard_map/dot_general | solution.py:143
  181.9 1.0 fusion.2
  182.9 1.2 convolution_convert_fusion.1
  184.2 0.7 pad_maximum_fusion.2
  185.0 5.8 %fusion.7 = f32[512,512]{0,1:T(8,128)S(1)} fusion(bf16[512,4096]{1,0:T(8,128)(2,1)} %all-gather.7.cloned.1.call-done, bf16[4096,512]{1,0:T(8,128)(2,1)} %param.12), kind=kOutput, calls=%fused_computation.24 | convolution fusion | flops 2147483648 | bytes 9437184 | tf_op jit(solution)/shard_map/dot_general | solution.py:143
  190.8 0.3 copy.19
  191.2 1.1 fusion.6
  192.3 1.4 copy.27
  193.7 2.4 copy.28
  196.1 1.9 maximum_multiply_fusion
  198.0 0.2 mul.63
  198.2 0.4 fusion.q_ref
  198.6 22.5 %all-gather.9.cloned.1.call-done.kv_ref = bf16[8192,256]{1,0:T(8,128)(2,1)} async-done(((bf16[512,256]{1,0:T(8,128)(2,1)}), bf16[8192,256]{1,0:T(8,128)(2,1)}) %all-gather.9.cloned.1.call-update) | async-done | bytes 4194320 | tf_op jit(solution)/shard_map/all_gather | solution.py:160
  221.1 2.2 copy-done.1
  223.3 8.4 %attend.1 = bf16[512,512]{1,0:T(8,128)(2,1)S(1)} custom-call(s32[4,64]{1,0:T(4,128)S(1)} %copy-done.2, bf16[512,512]{1,0:T(8,128)(2,1)S(1)} %fusion.q_ref, bf16[8192,256]{1,0:T(8,128)(2,1)S(1)} %copy-done.1), custom_call_target="tpu_custom_call" | custom-call | tf_op jit(solution)/shard_map/attend/pallas_call | solution.py:112
  231.8 4.3 %convolution_convert_fusion = bf16[512,4096]{1,0:T(8,128)(2,1)} fusion(bf16[512,512]{1,0:T(8,128)(2,1)S(1)} %attend.1, bf16[512,4096]{1,0:T(8,128)(2,1)S(1)} %copy-done.4), kind=kOutput, calls=%fused_computation.1 | convolution fusion | flops 2149580800 | bytes 8912896 | tf_op jit(solution)/shard_map/dot_general | solution.py:163
  236.1 86.4 %reduce-scatter.2.cloned.1.call-done = bf16[64,4096]{1,0:T(8,128)(2,1)} async-done(((bf16[512,4096]{1,0:T(8,128)(2,1)}), bf16[64,4096]{1,0:T(8,128)(2,1)}) %reduce-scatter.2.cloned.1.call-update) | async-done | bytes 524304 | tf_op jit(solution)/shard_map/reduce_scatter | solution.py:162
  (22 shorter events, 0.4 us)
Async XLA Ops:
  6.5 171.7 %copy-start = (bf16[4096,128]{1,0:T(8,128)(2,1)S(1)}, bf16[4096,128]{1,0:T(8,128)(2,1)}, u32[]{:S(2)}) copy-start(bf16[4096,128]{1,0:T(8,128)(2,1)} %param.13) | copy-start | bytes 3145732
  6.5 56.6 %all-gather.5.cloned.1.call-start = ((), (), s32[]{:S(2)}) async-start(), calls=%async_computation.1 | async-start | bytes 8912896 | tf_op jit(solution)/shard_map/all_gather | solution.py:134
  7.3 170.9 %all-gather.7.cloned.1.call-start = ((), (), s32[]{:S(2)}) async-start(), calls=%async_computation.2 | async-start | bytes 4718592 | tf_op jit(solution)/shard_map/all_gather | solution.py:140
  99.8 121.4 %all-gather.9.cloned.1.call-start = ((), (), s32[]{:S(2)}) async-start(), calls=%async_computation.3 | async-start | bytes 4456448 | tf_op jit(solution)/shard_map/all_gather | solution.py:160
  178.2 4.7 %copy-start.3 = (bf16[512,4096]{1,0:T(8,128)(2,1)S(1)}, bf16[512,4096]{1,0:T(8,128)(2,1)}, u32[]{:S(2)}) copy-start(bf16[512,4096]{1,0:T(8,128)(2,1)} %all-gather.7.cloned.1.call-done) | copy-start | bytes 12582916
  178.2 4.7 %copy-start.5 = (bf16[4096,128]{1,0:T(8,128)(2,1)S(1)}, bf16[4096,128]{1,0:T(8,128)(2,1)}, u32[]{:S(2)}) copy-start(bf16[4096,128]{1,0:T(8,128)(2,1)} %param.14) | copy-start | bytes 3145732
  184.9 137.6 %reduce-scatter.2.cloned.1.call-start = ((), (), s32[]{:S(2)}) async-start(), calls=%async_computation.4 | async-start | bytes 4718592 | tf_op jit(solution)/shard_map/reduce_scatter | solution.py:162
  196.1 25.0 %copy-start.2 = (s32[4,64]{1,0:T(4,128)S(1)}, s32[4,64]{1,0:T(4,128)}, u32[]{:S(2)}) copy-start(s32[4,64]{1,0:T(4,128)} %mask_ref.1) | copy-start | bytes 3076
  221.1 2.2 copy-start.1
  223.3 8.4 %copy-start.4 = (bf16[512,4096]{1,0:T(8,128)(2,1)S(1)}, bf16[512,4096]{1,0:T(8,128)(2,1)}, u32[]{:S(2)}) copy-start(bf16[512,4096]{1,0:T(8,128)(2,1)} %param.15) | copy-start | bytes 12582916
Sparse Core Ops, SparseCore 0:
  9.1 54.0 all-gather.4
  99.9 78.2 all-gather.6
  185.1 36.0 all-gather.8
  236.2 86.2 reduce-scatter.1

commit v2 on v1

--- a/solution.py
+++ b/solution.py
@@ -1,4 +1,3 @@
-import functools
 import math
 
 import jax
@@ -127,6 +126,178 @@
     )(block_mask, queries, kv)
 
 
+def ring_places():
+    head = lax.axis_index("head")
+    y, zh = head // 2, head % 2
+    up = ((y + 1) % 4) * 2 + zh
+    down = ((y + 3) % 4) * 2 + zh
+    across = y * 2 + (1 - zh)
+    return y, zh, up, down, across
+
+
+def remote(src, dst, send_sem, recv_sem, **place):
+    return pltpu.make_async_remote_copy(
+        src_ref=src,
+        dst_ref=dst,
+        send_sem=send_sem,
+        recv_sem=recv_sem,
+        device_id=place,
+        device_id_type=pl.DeviceIdType.MESH,
+    )
+
+
+OUT_CHUNKS = 4
+
+
+def project_out_kernel(
+    att_ref, w_hbm, out_ref, w_ref, part, far_out, far_in, near_out, near_in, z_out, z_in, w_sem,
+    far_ss, far_rs, near_ss, near_rs, z_ss, z_rs,
+):
+    y, zh, up, down, across = ring_places()
+    cw = part.shape[2]
+    half = cw // 2
+    loads = [
+        pltpu.make_async_copy(w_hbm.at[:, pl.ds(c * cw, cw)], w_ref.at[c], w_sem.at[c])
+        for c in range(OUT_CHUNKS)
+    ]
+    for load in loads:
+        load.start()
+    barrier = pltpu.get_barrier_semaphore()
+    for peer in (up, down, across):
+        pl.semaphore_signal(
+            barrier, inc=1, device_id={"head": peer}, device_id_type=pl.DeviceIdType.MESH
+        )
+    pl.semaphore_wait(barrier, 3)
+
+    def rows_of(c, place, lo):
+        return part[c, pl.ds(pl.multiple_of(place * 128, 128), 128), lo : lo + half]
+
+    def far(c, side):
+        return remote(
+            far_out.at[c, side], far_in.at[c, side], far_ss.at[c, side], far_rs.at[c, side],
+            head=(up, down)[side],
+        )
+
+    def near(c, side, part_at):
+        return remote(
+            near_out.at[c, side, part_at],
+            near_in.at[c, side, part_at],
+            near_ss.at[c, side, part_at],
+            near_rs.at[c, side, part_at],
+            head=(up, down)[side],
+        )
+
+    def cross(c):
+        return remote(z_out.at[c], z_in.at[c], z_ss.at[c], z_rs.at[c], head=across)
+
+    def first(c):
+        loads[c].wait()
+        part[c] = jnp.dot(att_ref[...], w_ref[c], preferred_element_type=jnp.float32)
+        for side in range(2):
+            far_out[c, side] = rows_of(c, (y + 2) % 4, side * half).astype(jnp.bfloat16)
+            far(c, side).start()
+        near_out[c, 0, 1] = rows_of(c, (y + 1) % 4, half).astype(jnp.bfloat16)
+        near(c, 0, 1).start()
+        near_out[c, 1, 0] = rows_of(c, (y + 3) % 4, 0).astype(jnp.bfloat16)
+        near(c, 1, 0).start()
+
+    def second(c):
+        far(c, 0).wait_recv()
+        near_out[c, 0, 0] = (
+            rows_of(c, (y + 1) % 4, 0) + far_in[c, 0].astype(jnp.float32)
+        ).astype(jnp.bfloat16)
+        near(c, 0, 0).start()
+        far(c, 1).wait_recv()
+        near_out[c, 1, 1] = (
+            rows_of(c, (y + 3) % 4, half) + far_in[c, 1].astype(jnp.float32)
+        ).astype(jnp.bfloat16)
+        near(c, 1, 1).start()
+
+    def third(c):
+        for side in range(2):
+            for at in range(2):
+                near(c, side, at).wait_recv()
+        mine = pl.multiple_of(y * 128, 128)
+        for at in range(2):
+            sl = slice(at * half, (at + 1) * half)
+            other = pl.ds(pl.multiple_of((1 - zh) * 64, 64), 64)
+            z_out[c, :, sl] = (
+                part[c, pl.ds(pl.multiple_of(mine + (1 - zh) * 64, 64), 64), sl]
+                + near_in[c, 0, at, other, :].astype(jnp.float32)
+                + near_in[c, 1, at, other, :].astype(jnp.float32)
+            ).astype(jnp.bfloat16)
+        cross(c).start()
+        for at in range(2):
+            sl = slice(at * half, (at + 1) * half)
+            own = pl.ds(pl.multiple_of(zh * 64, 64), 64)
+            place = pl.ds(pl.multiple_of(mine + zh * 64, 64), 64)
+            part[c, place, sl] = (
+                part[c, place, sl]
+                + near_in[c, 0, at, own, :].astype(jnp.float32)
+                + near_in[c, 1, at, own, :].astype(jnp.float32)
+            )
+
+    def fourth(c):
+        cross(c).wait_recv()
+        place = pl.ds(pl.multiple_of(y * 128 + zh * 64, 64), 64)
+        out_ref[:, c * cw : (c + 1) * cw] = (
+            part[c, place, :] + z_in[c].astype(jnp.float32)
+        ).astype(jnp.bfloat16)
+
+    first(0)
+    first(1)
+    for c in range(OUT_CHUNKS):
+        second(c)
+        if c + 2 < OUT_CHUNKS:
+            first(c + 2)
+    for c in range(OUT_CHUNKS):
+        third(c)
+    for c in range(OUT_CHUNKS):
+        fourth(c)
+    for c in range(OUT_CHUNKS):
+        for side in range(2):
+            far(c, side).wait_send()
+            for at in range(2):
+                near(c, side, at).wait_send()
+        cross(c).wait_send()
+
+
+def project_out(attended, w_out):
+    rows, depth = attended.shape
+    width = w_out.shape[1]
+    n, cw = OUT_CHUNKS, width // OUT_CHUNKS
+    half = cw // 2
+    bf16 = jnp.bfloat16
+    dma = pltpu.SemaphoreType.DMA
+    return pl.pallas_call(
+        project_out_kernel,
+        out_shape=jax.ShapeDtypeStruct((rows // 8, width), bf16),
+        in_specs=[pl.BlockSpec(memory_space=pltpu.VMEM), pl.BlockSpec(memory_space=pl.ANY)],
+        out_specs=pl.BlockSpec(memory_space=pltpu.VMEM),
+        scratch_shapes=[
+            pltpu.VMEM((n, depth, cw), bf16),
+            pltpu.VMEM((n, rows, cw), jnp.float32),
+            pltpu.VMEM((n, 2, rows // 4, half), bf16),
+            pltpu.VMEM((n, 2, rows // 4, half), bf16),
+            pltpu.VMEM((n, 2, 2, rows // 4, half), bf16),
+            pltpu.VMEM((n, 2, 2, rows // 4, half), bf16),
+            pltpu.VMEM((n, rows // 8, cw), bf16),
+            pltpu.VMEM((n, rows // 8, cw), bf16),
+            dma((n,)),
+            dma((n, 2)),
+            dma((n, 2)),
+            dma((n, 2, 2)),
+            dma((n, 2, 2)),
+            dma((n,)),
+            dma((n,)),
+        ],
+        compiler_params=pltpu.CompilerParams(
+            collective_id=1, has_side_effects=True, vmem_limit_bytes=48 * MIB
+        ),
+        name="project_out",
+    )(attended, w_out)
+
+
 def on_device(node_rows, node_target, node_position, block_mask, w_query, w_key, w_value, w_out):
     local_rows = node_rows.shape[0]
     row_offset = lax.axis_index("ctx") * local_rows
@@ -159,12 +330,7 @@
     kv_local = jnp.concatenate([rotate(key_proj), value_proj.astype(jnp.bfloat16)], axis=1)
     kv = lax.all_gather(kv_local, "ctx", axis=0, tiled=True)
     attended = attend(block_mask, queries, kv)
-    return lax.psum_scatter(
-        jnp.dot(attended, w_out, preferred_element_type=jnp.float32).astype(jnp.bfloat16),
-        "head",
-        scatter_dimension=0,
-        tiled=True,
-    )
+    return project_out(attended, w_out)
 
 
 def solution(mesh):

time: 331 us -> 287 us (0.87)
  waiting for transfers between devices: 225 us -> 139 us
  Pallas kernels: 8.42 us -> 55.1 us
  matrix products: 15 us -> 10.7 us
    reduce_scatter x1 -> x0, waiting for transfers between devices: 86.4 us -> none  [on_device(): lax.psum_scatter(jnp.dot(attended, w_out, preferred_element_type=jnp.floa...]
    pallas_call x0 -> x1, Pallas kernels: none -> 47.2 us  [project_out(): pl.pallas_call(project_out_kernel, out_shape=jax.ShapeDtypeStruct((rows /...]
    dot_general x1 -> x0, matrix products: 4.31 us -> none  [on_device(): jnp.dot(attended, w_out, preferred_element_type=jnp.float32)]
    unnamed x14 -> x15, local copies, waits for them, and re-layouts: 6 us -> 6.79 us
  transfers between devices with their start and end apart: 4 -> 3, of which waited for: 4 -> 3; matrix products, arithmetic and copies ran while one was open for 5% -> 5% of each run, Pallas kernels for 0% -> 0%
where the time goes in v2:
time: 287 us; the launch traced here: 286 us
  waiting for transfers between devices  139 us (48%)
  Pallas kernels  55.1 us (19%)
  local copies, waits for them, and re-layouts  45.1 us (16%)
  blocking collectives  16.9 us (6%)
  between operations  13.2 us (5%)
  matrix products  10.7 us (4%)
  other arithmetic  5.77 us (2%)
    all_gather x1, waiting for transfers between devices, on_device(): pieces_in = lax.all_gather(routed, 'head', axis=1, tiled=True)  76.7 us
    pallas_call x1, Pallas kernels, project_out(): pl.pallas_call(project_out_kernel, out_shape=jax.ShapeDtypeStruct((rows /...  47.2 us
    all_gather x1, waiting for transfers between devices, on_device(): lax.all_gather(node_rows, 'ctx', axis=0, tiled=True)  39 us
    scatter x1, local copies, waits for them, and re-layouts, on_device(): routed = jnp.zeros_like(node_rows).at[places].set(all_rows, mode='drop')  36.6 us
    all_gather x1, waiting for transfers between devices, on_device(): kv = lax.all_gather(kv_local, 'ctx', axis=0, tiled=True)  22.4 us
    all_gather x1, blocking collectives, on_device(): lax.all_gather(node_target, 'ctx', axis=0, tiled=True)  16.9 us
    dot_general x3, matrix products, on_device(): jnp.dot(pieces_in, weight, preferred_element_type=jnp.float32)  10.7 us
    pallas_call x1, Pallas kernels, attend(): pl.pallas_call(attend_kernel, out_shape=jax.ShapeDtypeStruct(queries.shap...  7.89 us
  transfers between devices with their start and end apart: 3, of which 3 were waited for; matrix products, arithmetic and copies ran while one was open for 5% of the time, Pallas kernels for 0%

profile of v2, /device:TPU:34, one launch (start us, length us, event | category | flops | bytes accessed | tf_op | source)
XLA Modules:
  0.0 285.6 jit_solution(15479139749462623359)
XLA Ops:
  6.5 0.7 all-gather.5.cloned.1.call-update
  7.3 16.9 %all-gather = s32[16,1,512]{2,1,0:T(1,128)S(1)} all-gather(s32[1,1,512]{2,1,0:T(1,128)} %bitcast.32), channel_id=1, replica_groups=mesh['ctx'=16,'head'=8] {'ctx'}, dimensions={0}, use_global_device_ids=true | all-gather | bytes 34816 | tf_op jit(solution)/shard_map/all_gather | solution.py:306
  24.2 39.0 %all-gather.5.cloned.1.call-done = bf16[8192,512]{1,0:T(8,128)(2,1)} async-done(((bf16[512,512]{1,0:T(8,128)(2,1)}), bf16[8192,512]{1,0:T(8,128)(2,1)}) %all-gather.5.cloned.1.call-update) | async-done | bytes 8388624 | tf_op jit(solution)/shard_map/all_gather | solution.py:305
  63.2 36.6 %scatter_custom_fusion = bf16[512,512]{1,0:T(8,128)(2,1)} fusion(s32[8192]{0:T(1024)S(1)} %compare_select_fusion, bf16[8192,512]{1,0:T(8,128)(2,1)} %all-gather.5.cloned.1.call-done, bf16[]{:T(256)} %constant.6.clone.1), kind=kCustom, calls=%fused_computation.16 | custom fusion | bytes 524800 | tf_op jit(solution)/shard_map/scatter | solution.py:310
  99.8 0.7 convert_element_type.14
  100.5 1.0 fusion.5
  101.5 76.7 %all-gather.7.cloned.1.call-done = bf16[512,4096]{1,0:T(8,128)(2,1)} async-done(((bf16[512,512]{1,0:T(8,128)(2,1)}), bf16[512,4096]{1,0:T(8,128)(2,1)}) %all-gather.7.cloned.1.call-update) | async-done | bytes 4194320 | tf_op jit(solution)/shard_map/all_gather | solution.py:311
  178.2 3.6 %fusion.8 = f32[512,128]{1,0:T(8,128)S(1)} fusion(bf16[512,4096]{1,0:T(8,128)(2,1)} %all-gather.7.cloned.1.call-done, bf16[4096,128]{1,0:T(8,128)(2,1)S(1)} %copy-done), kind=kOutput, calls=%fused_computation.24 | convolution fusion | flops 536870912 | bytes 5505024 | tf_op jit(solution)/shard_map/dot_general | solution.py:314
  181.9 1.0 fusion.2
  182.9 1.2 convolution_convert_fusion
  184.2 0.7 pad_maximum_fusion.2
  184.9 5.8 %fusion.7 = f32[512,512]{0,1:T(8,128)S(1)} fusion(bf16[512,4096]{1,0:T(8,128)(2,1)} %all-gather.7.cloned.1.call-done, bf16[4096,512]{1,0:T(8,128)(2,1)} %param.12), kind=kOutput, calls=%fused_computation.23 | convolution fusion | flops 2147483648 | bytes 9437184 | tf_op jit(solution)/shard_map/dot_general | solution.py:314
  190.8 0.3 copy.21
  191.1 1.1 fusion.6
  192.2 1.4 copy.29
  193.7 2.4 copy.30
  196.0 1.9 maximum_multiply_fusion
  198.0 0.2 mul.63
  198.2 0.4 fusion.q_ref
  198.6 22.4 %all-gather.9.cloned.1.call-done.kv_ref = bf16[8192,256]{1,0:T(8,128)(2,1)} async-done(((bf16[512,256]{1,0:T(8,128)(2,1)}), bf16[8192,256]{1,0:T(8,128)(2,1)}) %all-gather.9.cloned.1.call-update) | async-done | bytes 4194320 | tf_op jit(solution)/shard_map/all_gather | solution.py:331
  221.0 2.2 copy-done.2
  223.2 7.9 %attend.1.att_ref = bf16[512,512]{1,0:T(8,128)(2,1)S(1)} custom-call(s32[4,64]{1,0:T(4,128)S(1)} %copy-done.3, bf16[512,512]{1,0:T(8,128)(2,1)S(1)} %fusion.q_ref, bf16[8192,256]{1,0:T(8,128)(2,1)S(1)} %copy-done.2), custom_call_target="tpu_custom_call" | custom-call | tf_op jit(solution)/shard_map/attend/pallas_call | solution.py:111
  231.1 47.2 %project_out.1 = bf16[64,4096]{1,0:T(8,128)(2,1)S(1)} custom-call(bf16[512,512]{1,0:T(8,128)(2,1)S(1)} %attend.1.att_ref, bf16[512,4096]{1,0:T(8,128)(2,1)S(1)} %copy-done.1), custom_call_target="tpu_custom_call" | custom-call | tf_op jit(solution)/shard_map/project_out/pallas_call | solution.py:272
  278.3 0.8 copy.36
  (20 shorter events, 0.3 us)
Async XLA Ops:
  6.5 171.7 %copy-start = (bf16[4096,128]{1,0:T(8,128)(2,1)S(1)}, bf16[4096,128]{1,0:T(8,128)(2,1)}, u32[]{:S(2)}) copy-start(bf16[4096,128]{1,0:T(8,128)(2,1)} %param.13) | copy-start | bytes 3145732
  6.5 56.6 %all-gather.5.cloned.1.call-start = ((), (), s32[]{:S(2)}) async-start(), calls=%async_computation | async-start | bytes 8912896 | tf_op jit(solution)/shard_map/all_gather | solution.py:305
  7.3 170.9 %all-gather.7.cloned.1.call-start = ((), (), s32[]{:S(2)}) async-start(), calls=%async_computation.1 | async-start | bytes 4718592 | tf_op jit(solution)/shard_map/all_gather | solution.py:311
  99.8 121.3 %all-gather.9.cloned.1.call-start = ((), (), s32[]{:S(2)}) async-start(), calls=%async_computation.2 | async-start | bytes 4456448 | tf_op jit(solution)/shard_map/all_gather | solution.py:331
  178.2 4.7 %copy-start.4 = (bf16[512,4096]{1,0:T(8,128)(2,1)S(1)}, bf16[512,4096]{1,0:T(8,128)(2,1)}, u32[]{:S(2)}) copy-start(bf16[512,4096]{1,0:T(8,128)(2,1)} %all-gather.7.cloned.1.call-done) | copy-start | bytes 12582916
  178.2 4.7 %copy-start.5 = (bf16[4096,128]{1,0:T(8,128)(2,1)S(1)}, bf16[4096,128]{1,0:T(8,128)(2,1)}, u32[]{:S(2)}) copy-start(bf16[4096,128]{1,0:T(8,128)(2,1)} %param.14) | copy-start | bytes 3145732
  196.0 25.0 %copy-start.3 = (s32[4,64]{1,0:T(4,128)S(1)}, s32[4,64]{1,0:T(4,128)}, u32[]{:S(2)}) copy-start(s32[4,64]{1,0:T(4,128)} %mask_ref.1) | copy-start | bytes 3076
  221.0 2.2 copy-start.2
  223.2 7.9 %copy-start.1 = (bf16[512,4096]{1,0:T(8,128)(2,1)S(1)}, bf16[512,4096]{1,0:T(8,128)(2,1)}, u32[]{:S(2)}) copy-start(bf16[512,4096]{1,0:T(8,128)(2,1)} %w_hbm.1) | copy-start | bytes 12582916
Sparse Core Ops, SparseCore 0:
  9.1 54.0 all-gather.4
  99.9 78.2 all-gather.6
  185.1 35.8 all-gather.8

commit v3 on v2

--- a/solution.py
+++ b/solution.py
@@ -298,36 +298,247 @@
     )(attended, w_out)
 
 
+IN_CHUNKS = 2
+SLOTS = 64
+
+
+def gather_kernel(
+    target_ref, x_ref, cos_ref, sin_ref, wq_hbm, wk_hbm, wv_hbm, q_ref, kv_ref,
+    w_ref, pick, place, send, recv, meta_out, meta_in, pieces, acc,
+    w_sem, row_ss, row_rs, meta_ss, meta_rs, ag_ss, ag_rs,
+):
+    ctx = lax.axis_index("ctx")
+    peers = lax.axis_size("ctx")
+    rows, cols = x_ref.shape
+    chunk = cols // IN_CHUNKS
+    y, zh, up, down, across = ring_places()
+    own_piece = y * 2 + zh
+    bf16 = jnp.bfloat16
+    loads = [
+        pltpu.make_async_copy(wq_hbm, w_ref.at[:, 0:512], w_sem.at[0]),
+        pltpu.make_async_copy(wk_hbm, w_ref.at[:, 512:640], w_sem.at[1]),
+        pltpu.make_async_copy(wv_hbm, w_ref.at[:, 640:768], w_sem.at[2]),
+    ]
+    for load in loads:
+        load.start()
+    barrier = pltpu.get_barrier_semaphore()
+    for k in range(1, peers):
+        pl.semaphore_signal(
+            barrier, inc=1, device_id={"ctx": (ctx + k) % peers},
+            device_id_type=pl.DeviceIdType.MESH,
+        )
+    for peer in (up, down, across):
+        pl.semaphore_signal(
+            barrier, inc=1, device_id={"head": peer}, device_id_type=pl.DeviceIdType.MESH
+        )
+
+    target = target_ref[...]
+    owner = target // rows
+    local = target - owner * rows
+    owned = lax.broadcasted_iota(jnp.int32, (peers, rows), 0) == owner
+    owned_f = jnp.where(owned, 1.0, 0.0).astype(jnp.float32)
+    earlier = (
+        lax.broadcasted_iota(jnp.int32, (rows, rows), 0)
+        < lax.broadcasted_iota(jnp.int32, (rows, rows), 1)
+    )
+    before = jnp.dot(
+        owned_f.astype(bf16),
+        jnp.where(earlier, 1.0, 0.0).astype(bf16),
+        preferred_element_type=jnp.float32,
+    )
+    rank = jnp.sum(owned_f * before, axis=0, keepdims=True)
+    slot = owner * SLOTS + rank.astype(jnp.int32)
+    for i in range(peers):
+        at = lax.broadcasted_iota(jnp.int32, (SLOTS, rows), 0) + i * SLOTS
+        pick[i * SLOTS : (i + 1) * SLOTS, :] = jnp.where(at == slot, 1.0, 0.0).astype(bf16)
+    line = lax.broadcasted_iota(jnp.int32, (8, rows), 0)
+    high = local // 16
+    facts = jnp.where(line == 0, high, jnp.where(line == 1, local - high * 16, 1))
+    facts = lax.dot_general(
+        facts.astype(jnp.float32).astype(bf16), pick[...], (((1,), (1,)), ((), ())),
+        preferred_element_type=jnp.float32,
+    )
+    goes_to = jnp.where(facts[2:3] > 0.5, facts[0:1] * 16.0 + facts[1:2], -1.0)
+    goes_to = jnp.broadcast_to(goes_to, (8, peers * SLOTS))
+    for i in range(peers // 2):
+        tile = goes_to[:, i * 128 : (i + 1) * 128]
+        meta_out[2 * i] = tile
+        meta_out[2 * i + 1] = pltpu.roll(tile, SLOTS, 1)
+
+    def meta_copy(k):
+        to = (ctx + k) % peers
+        return remote(meta_out.at[to], meta_in.at[k], meta_ss.at[k], meta_rs.at[k], ctx=to)
+
+    def row_copy(f, k):
+        to = (ctx + k) % peers
+        return remote(
+            send.at[f, pl.ds(pl.multiple_of(to * SLOTS, SLOTS), SLOTS)],
+            recv.at[f, pl.ds(k * SLOTS, SLOTS)],
+            row_ss.at[f, k], row_rs.at[f, k], ctx=to,
+        )
+
+    for f in range(IN_CHUNKS):
+        send[f] = jnp.dot(
+            pick[...], x_ref[:, f * chunk : (f + 1) * chunk], preferred_element_type=jnp.float32
+        ).astype(bf16)
+        if f == 0:
+            pl.semaphore_wait(barrier, peers - 1 + 3)
+            for k in range(1, peers):
+                meta_copy(k).start()
+        for k in range(1, peers):
+            row_copy(f, k).start()
+        recv[f, 0:SLOTS, :] = send[f, pl.ds(pl.multiple_of(ctx * SLOTS, SLOTS), SLOTS), :]
+    meta_in[0] = meta_out[ctx]
+
+    for k in range(1, peers):
+        meta_copy(k).wait_recv()
+    lane = lax.broadcasted_iota(jnp.int32, (8, 128), 1)
+    for i in range(peers // 2):
+        both = jnp.where(lane < SLOTS, meta_in[2 * i], pltpu.roll(meta_in[2 * i + 1], SLOTS, 1))
+        both = both[0:1].astype(jnp.int32)
+        at = lax.broadcasted_iota(jnp.int32, (rows, 128), 0)
+        place[:, i * 128 : (i + 1) * 128] = jnp.where(at == both, 1.0, 0.0).astype(bf16)
+
+    half = rows // 2
+    piece = lambda dy, other: ((y + dy) % 4) * 2 + ((1 - zh) if other else zh)
+
+    def spread(f, e):
+        src, lo, n, to = (
+            (piece(0, 0), 0, rows, across),
+            (piece(0, 0), 0, rows, up),
+            (piece(0, 0), 0, rows, down),
+            (piece(3, 0), 0, half, up),
+            (piece(1, 0), half, half, down),
+            (piece(0, 1), 0, rows, up),
+            (piece(0, 1), 0, rows, down),
+            (piece(3, 1), 0, half, up),
+            (piece(1, 1), half, half, down),
+        )[e]
+        ref = pieces.at[src, f, pl.ds(lo, n)]
+        return remote(ref, ref, ag_ss.at[f, e], ag_rs.at[f, e], head=to)
+
+    def project(f, index, first=False):
+        deep = pl.ds(pl.multiple_of(index * cols + f * chunk, chunk), chunk)
+        term = jnp.dot(pieces[index, f], w_ref[deep, :], preferred_element_type=jnp.float32)
+        acc[...] = term if first else acc[...] + term
+
+    for f in range(IN_CHUNKS):
+        for k in range(1, peers):
+            row_copy(f, k).wait_recv()
+        pieces[own_piece, f] = jnp.dot(
+            place[...], recv[f], preferred_element_type=jnp.float32
+        ).astype(bf16)
+        for e in (0, 1, 2):
+            spread(f, e).start()
+    for load in loads:
+        load.wait()
+
+    def near(f):
+        project(f, own_piece, first=f == 0)
+        spread(f, 1).wait_recv()
+        spread(f, 3).start()
+        spread(f, 2).wait_recv()
+        spread(f, 4).start()
+        spread(f, 0).wait_recv()
+        spread(f, 5).start()
+        spread(f, 6).start()
+        project(f, piece(3, 0))
+        project(f, piece(1, 0))
+        project(f, piece(0, 1))
+
+    def far(f):
+        spread(f, 3).wait_recv()
+        spread(f, 4).wait_recv()
+        project(f, piece(2, 0))
+
+    def near_other(f):
+        spread(f, 5).wait_recv()
+        spread(f, 7).start()
+        spread(f, 6).wait_recv()
+        spread(f, 8).start()
+        project(f, piece(3, 1))
+        project(f, piece(1, 1))
+
+    def far_other(f):
+        spread(f, 7).wait_recv()
+        spread(f, 8).wait_recv()
+        project(f, piece(2, 1))
+
+    near(0)
+    near(1)
+    near_other(0)
+    far(0)
+    far(1)
+    near_other(1)
+    far_other(0)
+    far_other(1)
+
+    cosine, sine = cos_ref[...], sin_ref[...]
+    for h in range(6):
+        tensor = acc[:, h * HD : (h + 1) * HD]
+        if h < 5:
+            tensor = tensor * cosine + pltpu.roll(tensor, HD // 2, 1) * sine
+        tensor = tensor.astype(bf16)
+        if h < 4:
+            q_ref[:, h * HD : (h + 1) * HD] = tensor
+        else:
+            kv_ref[:, (h - 4) * HD : (h - 3) * HD] = tensor
+
+    for k in range(1, peers):
+        meta_copy(k).wait_send()
+        for f in range(IN_CHUNKS):
+            row_copy(f, k).wait_send()
+    for f in range(IN_CHUNKS):
+        for e in range(9):
+            spread(f, e).wait_send()
+
+
+def gather_and_project(node_rows, node_target, cosine, sine, w_query, w_key, w_value):
+    rows, cols = node_rows.shape
+    peers = lax.axis_size("ctx")
+    chunk = cols // IN_CHUNKS
+    bf16 = jnp.bfloat16
+    dma = pltpu.SemaphoreType.DMA
+    vmem = pl.BlockSpec(memory_space=pltpu.VMEM)
+    anywhere = pl.BlockSpec(memory_space=pl.ANY)
+    return pl.pallas_call(
+        gather_kernel,
+        out_shape=(
+            jax.ShapeDtypeStruct((rows, 512), bf16),
+            jax.ShapeDtypeStruct((rows, 256), bf16),
+        ),
+        in_specs=[vmem, vmem, vmem, vmem, anywhere, anywhere, anywhere],
+        out_specs=(vmem, vmem),
+        scratch_shapes=[
+            pltpu.VMEM((w_query.shape[0], 768), bf16),
+            pltpu.VMEM((peers * SLOTS, rows), bf16),
+            pltpu.VMEM((rows, peers * SLOTS), bf16),
+            pltpu.VMEM((IN_CHUNKS, peers * SLOTS, chunk), bf16),
+            pltpu.VMEM((IN_CHUNKS, peers * SLOTS, chunk), bf16),
+            pltpu.VMEM((peers, 8, 128), jnp.float32),
+            pltpu.VMEM((peers, 8, 128), jnp.float32),
+            pltpu.VMEM((8, IN_CHUNKS, rows, chunk), bf16),
+            pltpu.VMEM((rows, 768), jnp.float32),
+            dma((3,)),
+            dma((IN_CHUNKS, peers)),
+            dma((IN_CHUNKS, peers)),
+            dma((peers,)),
+            dma((peers,)),
+            dma((IN_CHUNKS, 9)),
+            dma((IN_CHUNKS, 9)),
+        ],
+        compiler_params=pltpu.CompilerParams(
+            collective_id=2, has_side_effects=True, vmem_limit_bytes=48 * MIB
+        ),
+        name="gather_and_project",
+    )(node_target.reshape(1, rows), node_rows, cosine, sine, w_query, w_key, w_value)
+
+
 def on_device(node_rows, node_target, node_position, block_mask, w_query, w_key, w_value, w_out):
-    local_rows = node_rows.shape[0]
-    row_offset = lax.axis_index("ctx") * local_rows
-    all_rows, all_targets = (
-        lax.all_gather(node_rows, "ctx", axis=0, tiled=True),
-        lax.all_gather(node_target, "ctx", axis=0, tiled=True),
-    )
-    places = all_targets - row_offset
-    places = jnp.where((places >= 0) & (places < local_rows), places, local_rows)
-    routed = jnp.zeros_like(node_rows).at[places].set(all_rows, mode="drop")
-    pieces_in = lax.all_gather(routed, "head", axis=1, tiled=True)
-    query_proj, key_proj, value_proj = tuple(
-        (
-            jnp.dot(pieces_in, weight, preferred_element_type=jnp.float32)
-            for weight in (w_query, w_key, w_value)
-        )
-    )
     cosine, sine = rotary_tables(node_position, HD)
-
-    def rotate(tensor):
-        heads = tensor.reshape(local_rows, -1, HD)
-        turned = jnp.roll(heads, HD // 2, axis=-1)
-        return (
-            (heads * cosine[:, None, :] + turned * sine[:, None, :])
-            .astype(jnp.bfloat16)
-            .reshape(tensor.shape)
-        )
-
-    queries = rotate(query_proj)
-    kv_local = jnp.concatenate([rotate(key_proj), value_proj.astype(jnp.bfloat16)], axis=1)
+    queries, kv_local = gather_and_project(
+        node_rows, node_target, cosine, sine, w_query, w_key, w_value
+    )
     kv = lax.all_gather(kv_local, "ctx", axis=0, tiled=True)
     attended = attend(block_mask, queries, kv)
     return project_out(attended, w_out)

time: 287 us -> 169 us (0.59)
  waiting for transfers between devices: 139 us -> 36.8 us
  Pallas kernels: 55.1 us -> 107 us
  local copies, waits for them, and re-layouts: 45.1 us -> 7.31 us
  blocking collectives: 16.9 us -> 0 us
  matrix products: 10.7 us -> 0 us
  other arithmetic: 5.77 us -> 1.89 us
    all_gather x2 -> x0, waiting for transfers between devices: 116 us -> none  [the longest x1 76.7 us: on_device(): pieces_in = lax.all_gather(routed, 'head', axis=1, tiled=True)]
    pallas_call x0 -> x1, Pallas kernels: none -> 53.6 us  [gather_and_project(): pl.pallas_call(gather_kernel, out_shape=(jax.ShapeDtypeStruct((rows, 512)...]
    scatter x1 -> x0, local copies, waits for them, and re-layouts: 36.6 us -> none  [on_device(): routed = jnp.zeros_like(node_rows).at[places].set(all_rows, mode='drop')]
    all_gather x1 -> x0, blocking collectives: 16.9 us -> none  [on_device(): lax.all_gather(node_target, 'ctx', axis=0, tiled=True)]
    all_gather x1, waiting for transfers between devices: 22.4 us -> 36.7 us  [on_device(): kv = lax.all_gather(kv_local, 'ctx', axis=0, tiled=True)]
    dot_general x3 -> x0, matrix products: 10.7 us -> none  [on_device(): jnp.dot(pieces_in, weight, preferred_element_type=jnp.float32)]
  transfers between devices with their start and end apart: 3 -> 1, of which waited for: 3 -> 1; matrix products, arithmetic and copies ran while one was open for 5% -> 0% of each run, Pallas kernels for 0% -> 0%
where the time goes in v3:
time: 169 us; the launch traced here: 166 us
  Pallas kernels  107 us (63%)
  waiting for transfers between devices  36.8 us (22%)
  between operations  13.5 us (8%)
  local copies, waits for them, and re-layouts  7.31 us (4%)
  other arithmetic  1.89 us (1%)
    pallas_call x1, Pallas kernels, gather_and_project(): pl.pallas_call(gather_kernel, out_shape=(jax.ShapeDtypeStruct((rows, 512)...  53.6 us
    pallas_call x1, Pallas kernels, project_out(): pl.pallas_call(project_out_kernel, out_shape=jax.ShapeDtypeStruct((rows /...  44.4 us
    all_gather x1, waiting for transfers between devices, on_device(): kv = lax.all_gather(kv_local, 'ctx', axis=0, tiled=True)  36.7 us
    pallas_call x1, Pallas kernels, attend(): pl.pallas_call(attend_kernel, out_shape=jax.ShapeDtypeStruct(queries.shap...  8.98 us
    unnamed x15, local copies, waits for them, and re-layouts  7.31 us
  transfers between devices with their start and end apart: 1, of which 1 were waited for; matrix products, arithmetic and copies ran while one was open for 0% of the time, Pallas kernels for 0%

profile of v3, /device:TPU:34, one launch (start us, length us, event | category | flops | bytes accessed | tf_op | source)
XLA Modules:
  0.0 166.4 jit_solution(16353634703468283807)
XLA Ops:
  6.5 0.0 all-gather.2.cloned.1.call-start
  6.5 0.7 convert_element_type.3
  7.2 1.0 fusion
  8.2 0.0 copy-start.5
  8.2 0.2 pad_maximum_fusion
  8.5 0.0 copy-start.2
  8.5 1.2 copy-done.2
  9.7 0.0 copy-start.3
  9.7 1.2 copy-done.3
  10.9 0.0 copy-start.4
  10.9 1.0 copy-done.4
  12.0 0.0 copy-start.6
  12.0 0.7 copy-done.6
  12.6 53.6 %gather_and_project.1 = (bf16[512,512]{1,0:T(8,128)(2,1)S(1)}, bf16[512,256]{1,0:T(8,128)(2,1)}) custom-call(s32[1,512]{1,0:T(1,128)S(1)} %bitcast.1, bf16[512,512]{1,0:T(8,128)(2,1)S(1)} %copy-done.4, f32[512,128]{1,0:T(8,128)S(1)} %get-tuple-element.12.cos_ref, f32[512,128]{1,0:T(8,128)S(1)} %get-tuple-element.13.sin_ref, bf16[4096,512]{1,0:T(8,128)(2,1)} %wq_hbm.1, ...), custom_call_target="tpu_custom_call" | custom-call | tf_op jit(solution)/shard_map/gather_and_project/pallas_call | solution.py:504
  66.2 0.0 all-gather.2.cloned.1.call-update
  66.3 36.7 %all-gather.2.cloned.1.call-done.kv_ref = bf16[8192,256]{1,0:T(8,128)(2,1)} async-done(((bf16[512,256]{1,0:T(8,128)(2,1)}), bf16[8192,256]{1,0:T(8,128)(2,1)}) %all-gather.2.cloned.1.call-update) | async-done | bytes 4194320 | tf_op jit(solution)/shard_map/all_gather | solution.py:542
  103.0 0.0 copy-start
  103.0 0.0 copy-done.5
  103.0 0.0 copy-start.1
  103.0 2.3 %copy-done.1 = bf16[8192,256]{1,0:T(8,128)(2,1)S(1)} copy-done((bf16[8192,256]{1,0:T(8,128)(2,1)S(1)}, bf16[8192,256]{1,0:T(8,128)(2,1)}, u32[]{:S(2)}) %copy-start.1) | copy-done | bytes 4194328
  105.4 9.0 %attend.1.att_ref = bf16[512,512]{1,0:T(8,128)(2,1)S(1)} custom-call(s32[4,64]{1,0:T(4,128)S(1)} %copy-done.5, bf16[512,512]{1,0:T(8,128)(2,1)S(1)} %get-tuple-element.7.q_ref, bf16[8192,256]{1,0:T(8,128)(2,1)S(1)} %copy-done.1), custom_call_target="tpu_custom_call" | custom-call | tf_op jit(solution)/shard_map/attend/pallas_call | solution.py:111
  114.4 0.0 copy-done
  114.4 44.4 %project_out.1 = bf16[64,4096]{1,0:T(8,128)(2,1)S(1)} custom-call(bf16[512,512]{1,0:T(8,128)(2,1)S(1)} %attend.1.att_ref, bf16[512,4096]{1,0:T(8,128)(2,1)S(1)} %copy-done), custom_call_target="tpu_custom_call" | custom-call | tf_op jit(solution)/shard_map/project_out/pallas_call | solution.py:272
  158.8 0.8 copy.10
  (1 shorter events, 0.0 us)
Async XLA Ops:
  6.5 96.5 %all-gather.2.cloned.1.call-start = ((), (), s32[]{:S(2)}) async-start(), calls=%async_computation | async-start | bytes 4456448 | tf_op jit(solution)/shard_map/all_gather | solution.py:542
  8.2 94.8 %copy-start.5 = (s32[4,64]{1,0:T(4,128)S(1)}, s32[4,64]{1,0:T(4,128)}, u32[]{:S(2)}) copy-start(s32[4,64]{1,0:T(4,128)} %mask_ref.1) | copy-start | bytes 3076
  8.5 1.2 copy-start.2
  9.7 1.2 copy-start.3
  10.9 1.0 copy-start.4
  12.0 0.7 copy-start.6
  103.0 11.3 %copy-start = (bf16[512,4096]{1,0:T(8,128)(2,1)S(1)}, bf16[512,4096]{1,0:T(8,128)(2,1)}, u32[]{:S(2)}) copy-start(bf16[512,4096]{1,0:T(8,128)(2,1)} %w_hbm.1) | copy-start | bytes 12582916
  103.0 2.3 %copy-start.1 = (bf16[8192,256]{1,0:T(8,128)(2,1)S(1)}, bf16[8192,256]{1,0:T(8,128)(2,1)}, u32[]{:S(2)}) copy-start(bf16[8192,256]{1,0:T(8,128)(2,1)} %all-gather.2.cloned.1.call-done.kv_ref) | copy-start | bytes 12582916
Sparse Core Ops, SparseCore 0:
  66.4 36.5 all-gather.1

commit v4 on v3

--- a/solution.py
+++ b/solution.py
@@ -298,26 +298,35 @@
     )(attended, w_out)
 
 
-IN_CHUNKS = 2
+IN_CHUNKS = 4
+PARTS = 2
 SLOTS = 64
 
 
 def gather_kernel(
-    target_ref, x_ref, cos_ref, sin_ref, wq_hbm, wk_hbm, wv_hbm, q_ref, kv_ref,
-    w_ref, pick, place, send, recv, meta_out, meta_in, pieces, acc,
-    w_sem, row_ss, row_rs, meta_ss, meta_rs, ag_ss, ag_rs,
+    target_ref, x_hbm, cos_hbm, sin_hbm, wq_hbm, wk_hbm, wv_hbm, q_ref, kv_ref,
+    x_ref, cos_ref, sin_ref, w_ref, pick, place, send, recv, meta_out, meta_in, pieces, acc,
+    kv_own, in_sem, row_ss, row_rs, meta_ss, meta_rs, ag_ss, ag_rs, kv_sem, kv_ss, kv_rs,
 ):
     ctx = lax.axis_index("ctx")
     peers = lax.axis_size("ctx")
     rows, cols = x_ref.shape
     chunk = cols // IN_CHUNKS
+    part_rows = rows // PARTS
     y, zh, up, down, across = ring_places()
-    own_piece = y * 2 + zh
     bf16 = jnp.bfloat16
     loads = [
-        pltpu.make_async_copy(wq_hbm, w_ref.at[:, 0:512], w_sem.at[0]),
-        pltpu.make_async_copy(wk_hbm, w_ref.at[:, 512:640], w_sem.at[1]),
-        pltpu.make_async_copy(wv_hbm, w_ref.at[:, 640:768], w_sem.at[2]),
+        pltpu.make_async_copy(src, dst, in_sem.at[i])
+        for i, (src, dst) in enumerate(
+            (
+                (x_hbm, x_ref),
+                (wq_hbm, w_ref.at[:, 0:512]),
+                (wk_hbm, w_ref.at[:, 512:640]),
+                (wv_hbm, w_ref.at[:, 640:768]),
+                (cos_hbm, cos_ref),
+                (sin_hbm, sin_ref),
+            )
+        )
     ]
     for load in loads:
         load.start()
@@ -351,19 +360,6 @@
     for i in range(peers):
         at = lax.broadcasted_iota(jnp.int32, (SLOTS, rows), 0) + i * SLOTS
         pick[i * SLOTS : (i + 1) * SLOTS, :] = jnp.where(at == slot, 1.0, 0.0).astype(bf16)
-    line = lax.broadcasted_iota(jnp.int32, (8, rows), 0)
-    high = local // 16
-    facts = jnp.where(line == 0, high, jnp.where(line == 1, local - high * 16, 1))
-    facts = lax.dot_general(
-        facts.astype(jnp.float32).astype(bf16), pick[...], (((1,), (1,)), ((), ())),
-        preferred_element_type=jnp.float32,
-    )
-    goes_to = jnp.where(facts[2:3] > 0.5, facts[0:1] * 16.0 + facts[1:2], -1.0)
-    goes_to = jnp.broadcast_to(goes_to, (8, peers * SLOTS))
-    for i in range(peers // 2):
-        tile = goes_to[:, i * 128 : (i + 1) * 128]
-        meta_out[2 * i] = tile
-        meta_out[2 * i + 1] = pltpu.roll(tile, SLOTS, 1)
 
     def meta_copy(k):
         to = (ctx + k) % peers
@@ -377,18 +373,33 @@
             row_ss.at[f, k], row_rs.at[f, k], ctx=to,
         )
 
+    loads[0].wait()
     for f in range(IN_CHUNKS):
         send[f] = jnp.dot(
             pick[...], x_ref[:, f * chunk : (f + 1) * chunk], preferred_element_type=jnp.float32
         ).astype(bf16)
         if f == 0:
             pl.semaphore_wait(barrier, peers - 1 + 3)
-            for k in range(1, peers):
-                meta_copy(k).start()
         for k in range(1, peers):
             row_copy(f, k).start()
         recv[f, 0:SLOTS, :] = send[f, pl.ds(pl.multiple_of(ctx * SLOTS, SLOTS), SLOTS), :]
-    meta_in[0] = meta_out[ctx]
+        if f == 0:
+            line = lax.broadcasted_iota(jnp.int32, (8, rows), 0)
+            high = local // 16
+            facts = jnp.where(line == 0, high, jnp.where(line == 1, local - high * 16, 1))
+            facts = lax.dot_general(
+                facts.astype(jnp.float32).astype(bf16), pick[...], (((1,), (1,)), ((), ())),
+                preferred_element_type=jnp.float32,
+            )
+            goes_to = jnp.where(facts[2:3] > 0.5, facts[0:1] * 16.0 + facts[1:2], -1.0)
+            goes_to = jnp.broadcast_to(goes_to, (8, peers * SLOTS))
+            for i in range(peers // 2):
+                tile = goes_to[:, i * 128 : (i + 1) * 128]
+                meta_out[2 * i] = tile
+                meta_out[2 * i + 1] = pltpu.roll(tile, SLOTS, 1)
+            for k in range(1, peers):
+                meta_copy(k).start()
+            meta_in[0] = meta_out[ctx]
 
     for k in range(1, peers):
         meta_copy(k).wait_recv()
@@ -399,117 +410,218 @@
         at = lax.broadcasted_iota(jnp.int32, (rows, 128), 0)
         place[:, i * 128 : (i + 1) * 128] = jnp.where(at == both, 1.0, 0.0).astype(bf16)
 
-    half = rows // 2
-    piece = lambda dy, other: ((y + dy) % 4) * 2 + ((1 - zh) if other else zh)
-
-    def spread(f, e):
-        src, lo, n, to = (
-            (piece(0, 0), 0, rows, across),
-            (piece(0, 0), 0, rows, up),
-            (piece(0, 0), 0, rows, down),
+    half = part_rows // 2
+
+    def piece(dy, other):
+        return ((y + dy) % 4) * 2 + ((1 - zh) if other else zh)
+
+    def spread(n, e):
+        part, f = divmod(n, IN_CHUNKS)
+        src, lo, size, to = (
+            (piece(0, 0), 0, part_rows, across),
+            (piece(0, 0), 0, part_rows, up),
+            (piece(0, 0), 0, part_rows, down),
             (piece(3, 0), 0, half, up),
             (piece(1, 0), half, half, down),
-            (piece(0, 1), 0, rows, up),
-            (piece(0, 1), 0, rows, down),
-            (piece(3, 1), 0, half, up),
-            (piece(1, 1), half, half, down),
+            (piece(0, 1), 0, part_rows, up),
+            (piece(0, 1), 0, part_rows, down),
+            (piece(2, 0), 0, part_rows, across),
         )[e]
-        ref = pieces.at[src, f, pl.ds(lo, n)]
-        return remote(ref, ref, ag_ss.at[f, e], ag_rs.at[f, e], head=to)
-
-    def project(f, index, first=False):
-        deep = pl.ds(pl.multiple_of(index * cols + f * chunk, chunk), chunk)
-        term = jnp.dot(pieces[index, f], w_ref[deep, :], preferred_element_type=jnp.float32)
-        acc[...] = term if first else acc[...] + term
-
-    for f in range(IN_CHUNKS):
-        for k in range(1, peers):
-            row_copy(f, k).wait_recv()
-        pieces[own_piece, f] = jnp.dot(
-            place[...], recv[f], preferred_element_type=jnp.float32
+        ref = pieces.at[src, part, f, pl.ds(lo, size)]
+        return remote(ref, ref, ag_ss.at[n, e], ag_rs.at[n, e], head=to)
+
+    def project(n, index, first=False):
+        part, f = divmod(n, IN_CHUNKS)
+        if f < IN_CHUNKS - 1:
+            return
+        piece_rows = jnp.concatenate(
+            [pieces[index, part, g] for g in range(IN_CHUNKS)], axis=1
+        )
+        deep = pl.ds(pl.multiple_of(index * cols, cols), cols)
+        term = jnp.dot(piece_rows, w_ref[deep, :], preferred_element_type=jnp.float32)
+        acc[part] = term if first else acc[part] + term
+
+    def begin(n):
+        part, f = divmod(n, IN_CHUNKS)
+        if part == 0:
+            for k in range(1, peers):
+                row_copy(f, k).wait_recv()
+        here = slice(part * part_rows, (part + 1) * part_rows)
+        pieces[piece(0, 0), part, f] = jnp.dot(
+            place[here, :], recv[f], preferred_element_type=jnp.float32
         ).astype(bf16)
-        for e in (0, 1, 2):
-            spread(f, e).start()
-    for load in loads:
-        load.wait()
-
-    def near(f):
-        project(f, own_piece, first=f == 0)
-        spread(f, 1).wait_recv()
-        spread(f, 3).start()
-        spread(f, 2).wait_recv()
-        spread(f, 4).start()
-        spread(f, 0).wait_recv()
-        spread(f, 5).start()
-        spread(f, 6).start()
-        project(f, piece(3, 0))
-        project(f, piece(1, 0))
-        project(f, piece(0, 1))
-
-    def far(f):
-        spread(f, 3).wait_recv()
-        spread(f, 4).wait_recv()
-        project(f, piece(2, 0))
-
-    def near_other(f):
-        spread(f, 5).wait_recv()
-        spread(f, 7).start()
-        spread(f, 6).wait_recv()
-        spread(f, 8).start()
-        project(f, piece(3, 1))
-        project(f, piece(1, 1))
-
-    def far_other(f):
-        spread(f, 7).wait_recv()
-        spread(f, 8).wait_recv()
-        project(f, piece(2, 1))
-
-    near(0)
-    near(1)
-    near_other(0)
-    far(0)
-    far(1)
-    near_other(1)
-    far_other(0)
-    far_other(1)
-
-    cosine, sine = cos_ref[...], sin_ref[...]
-    for h in range(6):
-        tensor = acc[:, h * HD : (h + 1) * HD]
-        if h < 5:
-            tensor = tensor * cosine + pltpu.roll(tensor, HD // 2, 1) * sine
-        tensor = tensor.astype(bf16)
-        if h < 4:
-            q_ref[:, h * HD : (h + 1) * HD] = tensor
+        for e in (1, 2, 0):
+            spread(n, e).start()
+        if n == IN_CHUNKS - 1:
+            for load in loads[1:]:
+                load.wait()
+        project(n, piece(0, 0), first=True)
+
+    def near(n):
+        spread(n, 1).wait_recv()
+        spread(n, 3).start()
+        spread(n, 2).wait_recv()
+        spread(n, 4).start()
+        spread(n, 0).wait_recv()
+        spread(n, 5).start()
+        spread(n, 6).start()
+        project(n, piece(3, 0))
+        project(n, piece(1, 0))
+        project(n, piece(0, 1))
+
+    def far(n):
+        spread(n, 3).wait_recv()
+        spread(n, 4).wait_recv()
+        spread(n, 7).start()
+        project(n, piece(2, 0))
+
+    def other(n):
+        spread(n, 5).wait_recv()
+        spread(n, 6).wait_recv()
+        project(n, piece(3, 1))
+        project(n, piece(1, 1))
+        spread(n, 7).wait_recv()
+        project(n, piece(2, 1))
+
+    zl, x, core = ctx // 8, (ctx // 2) % 4, ctx % 2
+    kv_half = part_rows // 2
+
+    def block(dx, other_z, other_core=0):
+        z = (1 - zl) if other_z else zl
+        c = (1 - core) if other_core else core
+        return z * 8 + ((x + dx) % 4) * 2 + c
+
+    kv_pieces = ((0, 0), (0, 1), (3, 0), (1, 0), (2, 0), (3, 1), (1, 1), (2, 1))
+
+    def share(part, e):
+        right, left, over = block(1, 0), block(3, 0), block(0, 1)
+        if e >= 8:
+            src, lo, size, to = block(*kv_pieces[e - 8]), 0, part_rows, block(0, 0, 1)
         else:
-            kv_ref[:, (h - 4) * HD : (h - 3) * HD] = tensor
+            src, lo, size, to = (
+                (block(0, 0), 0, part_rows, over),
+                (block(0, 0), 0, part_rows, right),
+                (block(0, 0), 0, part_rows, left),
+                (block(3, 0), 0, kv_half, right),
+                (block(1, 0), kv_half, kv_half, left),
+                (block(0, 1), 0, part_rows, right),
+                (block(0, 1), 0, part_rows, left),
+                (block(2, 0), 0, part_rows, over),
+            )[e]
+        ref = kv_ref.at[
+            pl.ds(pl.multiple_of(src * rows + part * part_rows + lo, 16), size)
+        ]
+        source = kv_own.at[part] if e in (0, 1, 2, 8) else ref
+        return remote(source, ref, kv_ss.at[part, e], kv_rs.at[part, e], ctx=to)
+
+    def keep(part):
+        at = pl.ds(pl.multiple_of(ctx * rows + part * part_rows, 16), part_rows)
+        return pltpu.make_async_copy(kv_own.at[part], kv_ref.at[at], kv_sem.at[part])
+
+    def finish(part):
+        here = slice(part * part_rows, (part + 1) * part_rows)
+        cosine, sine = cos_ref[here, :], sin_ref[here, :]
+        for h in (4, 5, 0, 1, 2, 3):
+            tensor = acc[part, :, h * HD : (h + 1) * HD]
+            if h < 5:
+                tensor = tensor * cosine + pltpu.roll(tensor, HD // 2, 1) * sine
+            tensor = tensor.astype(bf16)
+            if h < 4:
+                q_ref[here, h * HD : (h + 1) * HD] = tensor
+            else:
+                kv_own[part, :, (h - 4) * HD : (h - 3) * HD] = tensor
+            if h == 5:
+                for e in (1, 2, 0, 8):
+                    share(part, e).start()
+                keep(part).start()
+
+    def share_near(part):
+        share(part, 1).wait_recv()
+        share(part, 3).start()
+        share(part, 10).start()
+        share(part, 2).wait_recv()
+        share(part, 4).start()
+        share(part, 11).start()
+        share(part, 0).wait_recv()
+        share(part, 5).start()
+        share(part, 6).start()
+        share(part, 9).start()
+
+    def share_far(part):
+        share(part, 3).wait_recv()
+        share(part, 4).wait_recv()
+        share(part, 7).start()
+        share(part, 12).start()
+
+    def share_other(part):
+        share(part, 5).wait_recv()
+        share(part, 13).start()
+        share(part, 6).wait_recv()
+        share(part, 14).start()
+        share(part, 7).wait_recv()
+        share(part, 15).start()
+
+    count = IN_CHUNKS * PARTS
+    begin(0)
+    begin(1)
+    for n in range(count + 2):
+        if n < count:
+            near(n)
+        if n + 2 < count:
+            begin(n + 2)
+        if 1 <= n <= count:
+            far(n - 1)
+        if n >= 2:
+            other(n - 2)
+        if n == IN_CHUNKS + 1:
+            finish(0)
+        if n == IN_CHUNKS + 2:
+            share_near(0)
+        if n == IN_CHUNKS + 3:
+            share_far(0)
+    finish(1)
+    share_other(0)
+    share_near(1)
+    share_far(1)
+    share_other(1)
+    for part in range(PARTS):
+        for e in range(8, 16):
+            share(part, e).wait_recv()
 
     for k in range(1, peers):
         meta_copy(k).wait_send()
         for f in range(IN_CHUNKS):
             row_copy(f, k).wait_send()
-    for f in range(IN_CHUNKS):
-        for e in range(9):
-            spread(f, e).wait_send()
+    for n in range(count):
+        for e in range(8):
+            spread(n, e).wait_send()
+    for part in range(PARTS):
+        keep(part).wait()
+        for e in range(16):
+            share(part, e).wait_send()
 
 
 def gather_and_project(node_rows, node_target, cosine, sine, w_query, w_key, w_value):
     rows, cols = node_rows.shape
     peers = lax.axis_size("ctx")
     chunk = cols // IN_CHUNKS
+    part_rows = rows // PARTS
     bf16 = jnp.bfloat16
     dma = pltpu.SemaphoreType.DMA
     vmem = pl.BlockSpec(memory_space=pltpu.VMEM)
-    anywhere = pl.BlockSpec(memory_space=pl.ANY)
+    hbm = pl.BlockSpec(memory_space=pltpu.HBM)
     return pl.pallas_call(
         gather_kernel,
         out_shape=(
             jax.ShapeDtypeStruct((rows, 512), bf16),
-            jax.ShapeDtypeStruct((rows, 256), bf16),
+            jax.ShapeDtypeStruct((rows * peers, 256), bf16),
         ),
-        in_specs=[vmem, vmem, vmem, vmem, anywhere, anywhere, anywhere],
-        out_specs=(vmem, vmem),
+        in_specs=[vmem] + [hbm] * 6,
+        out_specs=(vmem, hbm),
         scratch_shapes=[
+            pltpu.VMEM((rows, cols), bf16),
+            pltpu.VMEM((rows, HD), jnp.float32),
+            pltpu.VMEM((rows, HD), jnp.float32),
             pltpu.VMEM((w_query.shape[0], 768), bf16),
             pltpu.VMEM((peers * SLOTS, rows), bf16),
             pltpu.VMEM((rows, peers * SLOTS), bf16),
@@ -517,15 +629,19 @@
             pltpu.VMEM((IN_CHUNKS, peers * SLOTS, chunk), bf16),
             pltpu.VMEM((peers, 8, 128), jnp.float32),
             pltpu.VMEM((peers, 8, 128), jnp.float32),
-            pltpu.VMEM((8, IN_CHUNKS, rows, chunk), bf16),
-            pltpu.VMEM((rows, 768), jnp.float32),
-            dma((3,)),
+            pltpu.VMEM((8, PARTS, IN_CHUNKS, part_rows, chunk), bf16),
+            pltpu.VMEM((PARTS, part_rows, 768), jnp.float32),
+            pltpu.VMEM((PARTS, part_rows, 256), bf16),
+            dma((6,)),
             dma((IN_CHUNKS, peers)),
             dma((IN_CHUNKS, peers)),
             dma((peers,)),
             dma((peers,)),
-            dma((IN_CHUNKS, 9)),
-            dma((IN_CHUNKS, 9)),
+            dma((PARTS * IN_CHUNKS, 8)),
+            dma((PARTS * IN_CHUNKS, 8)),
+            dma((PARTS,)),
+            dma((PARTS, 16)),
+            dma((PARTS, 16)),
         ],
         compiler_params=pltpu.CompilerParams(
             collective_id=2, has_side_effects=True, vmem_limit_bytes=48 * MIB
@@ -536,10 +652,9 @@
 
 def on_device(node_rows, node_target, node_position, block_mask, w_query, w_key, w_value, w_out):
     cosine, sine = rotary_tables(node_position, HD)
-    queries, kv_local = gather_and_project(
+    queries, kv = gather_and_project(
         node_rows, node_target, cosine, sine, w_query, w_key, w_value
     )
-    kv = lax.all_gather(kv_local, "ctx", axis=0, tiled=True)
     attended = attend(block_mask, queries, kv)
     return project_out(attended, w_out)
 

time: 169 us -> 140 us (0.83)
  waiting for transfers between devices: 36.8 us -> 0 us
  Pallas kernels: 107 us -> 129 us
  between operations: 13.5 us -> 0.09 us
    all_gather x1 -> x0, waiting for transfers between devices: 36.7 us -> none  [on_device(): kv = lax.all_gather(kv_local, 'ctx', axis=0, tiled=True)]
    pallas_call x1, Pallas kernels: 53.6 us -> 75.1 us  [gather_and_project(): pl.pallas_call(gather_kernel, out_shape=(jax.ShapeDtypeStruct((rows, 512)...]
    pallas_call x1, Pallas kernels: 44.4 us -> 46.3 us  [project_out(): pl.pallas_call(project_out_kernel, out_shape=jax.ShapeDtypeStruct((rows /...]
  transfers between devices with their start and end apart: 1 -> 0, of which waited for: 1 -> 0; matrix products, arithmetic and copies ran while one was open for 0% -> 0% of each run, Pallas kernels for 0% -> 0%
where the time goes in v4:
time: 140 us; the launch traced here: 139 us
  Pallas kernels  129 us (92%)
  local copies, waits for them, and re-layouts  7.31 us (5%)
  other arithmetic  1.89 us (1%)
    pallas_call x1, Pallas kernels, gather_and_project(): pl.pallas_call(gather_kernel, out_shape=(jax.ShapeDtypeStruct((rows, 512)...  75.1 us
    pallas_call x1, Pallas kernels, project_out(): pl.pallas_call(project_out_kernel, out_shape=jax.ShapeDtypeStruct((rows /...  46.3 us
    pallas_call x1, Pallas kernels, attend(): pl.pallas_call(attend_kernel, out_shape=jax.ShapeDtypeStruct(queries.shap...  7.89 us
    unnamed x15, local copies, waits for them, and re-layouts  7.31 us

profile of v4, /device:TPU:34, one launch (start us, length us, event | category | flops | bytes accessed | tf_op | source)
XLA Modules:
  0.0 138.6 jit_solution(10787516195519883143)
XLA Ops:
  0.0 0.7 convert_element_type.3
  0.7 1.0 fusion
  1.7 0.0 copy-start.5
  1.7 0.2 pad_maximum_fusion
  1.9 0.0 copy-start.2
  1.9 1.2 copy-done.2
  3.1 0.0 copy-start.3
  3.1 1.2 copy-done.3
  4.4 0.0 copy-start.4
  4.4 1.0 copy-done.4
  5.4 0.0 copy-start.6
  5.4 0.7 copy-done.6
  6.1 75.1 %gather_and_project.1 = (bf16[512,512]{1,0:T(8,128)(2,1)S(1)}, bf16[8192,256]{1,0:T(8,128)(2,1)}) custom-call(s32[1,512]{1,0:T(1,128)S(1)} %bitcast.1, bf16[512,512]{1,0:T(8,128)(2,1)S(1)} %copy-done.4, f32[512,128]{1,0:T(8,128)S(1)} %get-tuple-element.12.cos_hbm, f32[512,128]{1,0:T(8,128)S(1)} %get-tuple-element.13.sin_hbm, bf16[4096,512]{1,0:T(8,128)(2,1)} %wq_hbm.1, ...), custom_call_target="tpu_custom_call" | custom-call | tf_op jit(solution)/shard_map/gather_and_project/pallas_call | solution.py:613
  81.2 0.0 copy-start
  81.2 0.0 copy-done.5
  81.2 0.0 copy-start.1
  81.2 2.3 %copy-done.1 = bf16[8192,256]{1,0:T(8,128)(2,1)S(1)} copy-done((bf16[8192,256]{1,0:T(8,128)(2,1)S(1)}, bf16[8192,256]{1,0:T(8,128)(2,1)}, u32[]{:S(2)}) %copy-start.1) | copy-done | bytes 4194328
  83.6 7.9 %attend.1.att_ref = bf16[512,512]{1,0:T(8,128)(2,1)S(1)} custom-call(s32[4,64]{1,0:T(4,128)S(1)} %copy-done.5, bf16[512,512]{1,0:T(8,128)(2,1)S(1)} %get-tuple-element.7.q_ref, bf16[8192,256]{1,0:T(8,128)(2,1)S(1)} %copy-done.1), custom_call_target="tpu_custom_call" | custom-call | tf_op jit(solution)/shard_map/attend/pallas_call | solution.py:111
  91.5 0.0 copy-done
  91.5 46.3 %project_out.1 = bf16[64,4096]{1,0:T(8,128)(2,1)S(1)} custom-call(bf16[512,512]{1,0:T(8,128)(2,1)S(1)} %attend.1.att_ref, bf16[512,4096]{1,0:T(8,128)(2,1)S(1)} %copy-done), custom_call_target="tpu_custom_call" | custom-call | tf_op jit(solution)/shard_map/project_out/pallas_call | solution.py:272
  137.8 0.8 copy.10
  (1 shorter events, 0.0 us)
Async XLA Ops:
  1.7 79.5 %copy-start.5 = (s32[4,64]{1,0:T(4,128)S(1)}, s32[4,64]{1,0:T(4,128)}, u32[]{:S(2)}) copy-start(s32[4,64]{1,0:T(4,128)} %mask_ref.1) | copy-start | bytes 3076
  1.9 1.2 copy-start.2
  3.1 1.2 copy-start.3
  4.4 1.0 copy-start.4
  5.4 0.7 copy-start.6
  81.2 10.3 %copy-start = (bf16[512,4096]{1,0:T(8,128)(2,1)S(1)}, bf16[512,4096]{1,0:T(8,128)(2,1)}, u32[]{:S(2)}) copy-start(bf16[512,4096]{1,0:T(8,128)(2,1)} %w_hbm.1) | copy-start | bytes 12582916
  81.2 2.3 %copy-start.1 = (bf16[8192,256]{1,0:T(8,128)(2,1)S(1)}, bf16[8192,256]{1,0:T(8,128)(2,1)}, u32[]{:S(2)}) copy-start(bf16[8192,256]{1,0:T(8,128)(2,1)} %get-tuple-element.8.kv_ref) | copy-start | bytes 12582916

commit v5 on v4

--- a/solution.py
+++ b/solution.py
@@ -121,7 +121,7 @@
             pltpu.SMEM((128,), jnp.int32),
             pltpu.VMEM((HD, queries.shape[1]), jnp.float32),
         ],
-        compiler_params=pltpu.CompilerParams(vmem_limit_bytes=32 * MIB),
+        compiler_params=pltpu.CompilerParams(vmem_limit_bytes=60 * MIB),
         name="attend",
     )(block_mask, queries, kv)
 
@@ -146,16 +146,17 @@
     )
 
 
-OUT_CHUNKS = 4
+OUT_CHUNKS = 8
 
 
 def project_out_kernel(
-    att_ref, w_hbm, out_ref, w_ref, part, far_out, far_in, near_out, near_in, z_out, z_in, w_sem,
-    far_ss, far_rs, near_ss, near_rs, z_ss, z_rs,
+    att_ref, w_hbm, out_ref, w_ref, part, far_out, far_in, near_out, near_in, other_out, other_in,
+    z_out, z_in, w_sem, far_ss, far_rs, near_ss, near_rs, other_ss, other_rs, z_ss, z_rs,
 ):
     y, zh, up, down, across = ring_places()
     cw = part.shape[2]
     half = cw // 2
+    seat = part.shape[1] // 8
     loads = [
         pltpu.make_async_copy(w_hbm.at[:, pl.ds(c * cw, cw)], w_ref.at[c], w_sem.at[c])
         for c in range(OUT_CHUNKS)
@@ -167,10 +168,12 @@
         pl.semaphore_signal(
             barrier, inc=1, device_id={"head": peer}, device_id_type=pl.DeviceIdType.MESH
         )
-    pl.semaphore_wait(barrier, 3)
-
-    def rows_of(c, place, lo):
-        return part[c, pl.ds(pl.multiple_of(place * 128, 128), 128), lo : lo + half]
+
+    def rows_of(c, dy, other, lo=0, size=None):
+        index = ((y + dy) % 4) * 2 + ((1 - zh) if other else zh)
+        return part[
+            c, pl.ds(pl.multiple_of(index * seat, seat), seat), lo : lo + (size or cw)
+        ]
 
     def far(c, side):
         return remote(
@@ -178,88 +181,100 @@
             head=(up, down)[side],
         )
 
-    def near(c, side, part_at):
+    def near(c, side, at):
         return remote(
-            near_out.at[c, side, part_at],
-            near_in.at[c, side, part_at],
-            near_ss.at[c, side, part_at],
-            near_rs.at[c, side, part_at],
+            near_out.at[c, side, at], near_in.at[c, side, at],
+            near_ss.at[c, side, at], near_rs.at[c, side, at],
             head=(up, down)[side],
         )
 
-    def cross(c):
-        return remote(z_out.at[c], z_in.at[c], z_ss.at[c], z_rs.at[c], head=across)
+    def other(c, side):
+        return remote(
+            other_out.at[c, side], other_in.at[c, side], other_ss.at[c, side],
+            other_rs.at[c, side], head=(up, down)[side],
+        )
+
+    def cross(c, which):
+        return remote(
+            z_out.at[c, which], z_in.at[c, which], z_ss.at[c, which], z_rs.at[c, which],
+            head=across,
+        )
+
+    f32, bf16 = jnp.float32, jnp.bfloat16
 
     def first(c):
         loads[c].wait()
-        part[c] = jnp.dot(att_ref[...], w_ref[c], preferred_element_type=jnp.float32)
+        part[c] = jnp.dot(att_ref[...], w_ref[c], preferred_element_type=f32)
+        if c == 0:
+            pl.semaphore_wait(barrier, 3)
+        z_out[c, 0] = rows_of(c, 2, True).astype(bf16)
+        cross(c, 0).start()
+        for side, dy in ((0, 1), (1, 3)):
+            other_out[c, side] = rows_of(c, dy, True).astype(bf16)
+            other(c, side).start()
+        near_out[c, 0, 1] = rows_of(c, 1, False, half, half).astype(bf16)
+        near(c, 0, 1).start()
+        near_out[c, 1, 0] = rows_of(c, 3, False, 0, half).astype(bf16)
+        near(c, 1, 0).start()
+
+    def second(c):
+        cross(c, 0).wait_recv()
         for side in range(2):
-            far_out[c, side] = rows_of(c, (y + 2) % 4, side * half).astype(jnp.bfloat16)
+            far_out[c, side] = (
+                rows_of(c, 2, False, side * half, half)
+                + z_in[c, 0, :, side * half : (side + 1) * half].astype(f32)
+            ).astype(bf16)
             far(c, side).start()
-        near_out[c, 0, 1] = rows_of(c, (y + 1) % 4, half).astype(jnp.bfloat16)
-        near(c, 0, 1).start()
-        near_out[c, 1, 0] = rows_of(c, (y + 3) % 4, 0).astype(jnp.bfloat16)
-        near(c, 1, 0).start()
-
-    def second(c):
-        far(c, 0).wait_recv()
-        near_out[c, 0, 0] = (
-            rows_of(c, (y + 1) % 4, 0) + far_in[c, 0].astype(jnp.float32)
-        ).astype(jnp.bfloat16)
-        near(c, 0, 0).start()
-        far(c, 1).wait_recv()
-        near_out[c, 1, 1] = (
-            rows_of(c, (y + 3) % 4, half) + far_in[c, 1].astype(jnp.float32)
-        ).astype(jnp.bfloat16)
-        near(c, 1, 1).start()
 
     def third(c):
+        for side, dy in ((0, 1), (1, 3)):
+            far(c, side).wait_recv()
+            near_out[c, side, side] = (
+                rows_of(c, dy, False, side * half, half) + far_in[c, side].astype(f32)
+            ).astype(bf16)
+            near(c, side, side).start()
+
+    def fourth(c):
+        other(c, 0).wait_recv()
+        other(c, 1).wait_recv()
+        z_out[c, 1] = (
+            rows_of(c, 0, True) + other_in[c, 0].astype(f32) + other_in[c, 1].astype(f32)
+        ).astype(bf16)
+        cross(c, 1).start()
+
+    def fifth(c):
         for side in range(2):
             for at in range(2):
                 near(c, side, at).wait_recv()
-        mine = pl.multiple_of(y * 128, 128)
+        cross(c, 1).wait_recv()
         for at in range(2):
-            sl = slice(at * half, (at + 1) * half)
-            other = pl.ds(pl.multiple_of((1 - zh) * 64, 64), 64)
-            z_out[c, :, sl] = (
-                part[c, pl.ds(pl.multiple_of(mine + (1 - zh) * 64, 64), 64), sl]
-                + near_in[c, 0, at, other, :].astype(jnp.float32)
-                + near_in[c, 1, at, other, :].astype(jnp.float32)
-            ).astype(jnp.bfloat16)
-        cross(c).start()
-        for at in range(2):
-            sl = slice(at * half, (at + 1) * half)
-            own = pl.ds(pl.multiple_of(zh * 64, 64), 64)
-            place = pl.ds(pl.multiple_of(mine + zh * 64, 64), 64)
-            part[c, place, sl] = (
-                part[c, place, sl]
-                + near_in[c, 0, at, own, :].astype(jnp.float32)
-                + near_in[c, 1, at, own, :].astype(jnp.float32)
-            )
-
-    def fourth(c):
-        cross(c).wait_recv()
-        place = pl.ds(pl.multiple_of(y * 128 + zh * 64, 64), 64)
-        out_ref[:, c * cw : (c + 1) * cw] = (
-            part[c, place, :] + z_in[c].astype(jnp.float32)
-        ).astype(jnp.bfloat16)
+            here = slice(at * half, (at + 1) * half)
+            out_ref[:, c * cw + at * half : c * cw + (at + 1) * half] = (
+                rows_of(c, 0, False, at * half, half)
+                + near_in[c, 0, at].astype(f32)
+                + near_in[c, 1, at].astype(f32)
+                + z_in[c, 1, :, here].astype(f32)
+            ).astype(bf16)
 
     first(0)
     first(1)
-    for c in range(OUT_CHUNKS):
-        second(c)
-        if c + 2 < OUT_CHUNKS:
-            first(c + 2)
-    for c in range(OUT_CHUNKS):
-        third(c)
-    for c in range(OUT_CHUNKS):
-        fourth(c)
+    for n in range(OUT_CHUNKS + 3):
+        if n < OUT_CHUNKS:
+            second(n)
+        if n + 2 < OUT_CHUNKS:
+            first(n + 2)
+        if 1 <= n <= OUT_CHUNKS:
+            third(n - 1)
+            fourth(n - 1)
+        if n >= 3:
+            fifth(n - 3)
     for c in range(OUT_CHUNKS):
         for side in range(2):
             far(c, side).wait_send()
+            other(c, side).wait_send()
+            cross(c, side).wait_send()
             for at in range(2):
                 near(c, side, at).wait_send()
-        cross(c).wait_send()
 
 
 def project_out(attended, w_out):
@@ -267,32 +282,40 @@
     width = w_out.shape[1]
     n, cw = OUT_CHUNKS, width // OUT_CHUNKS
     half = cw // 2
+    seat = rows // 8
     bf16 = jnp.bfloat16
     dma = pltpu.SemaphoreType.DMA
     return pl.pallas_call(
         project_out_kernel,
-        out_shape=jax.ShapeDtypeStruct((rows // 8, width), bf16),
-        in_specs=[pl.BlockSpec(memory_space=pltpu.VMEM), pl.BlockSpec(memory_space=pl.ANY)],
+        out_shape=jax.ShapeDtypeStruct((seat, width), bf16),
+        in_specs=[
+            pl.BlockSpec(memory_space=pltpu.VMEM),
+            pl.BlockSpec(memory_space=pltpu.HBM),
+        ],
         out_specs=pl.BlockSpec(memory_space=pltpu.VMEM),
         scratch_shapes=[
             pltpu.VMEM((n, depth, cw), bf16),
             pltpu.VMEM((n, rows, cw), jnp.float32),
-            pltpu.VMEM((n, 2, rows // 4, half), bf16),
-            pltpu.VMEM((n, 2, rows // 4, half), bf16),
-            pltpu.VMEM((n, 2, 2, rows // 4, half), bf16),
-            pltpu.VMEM((n, 2, 2, rows // 4, half), bf16),
-            pltpu.VMEM((n, rows // 8, cw), bf16),
-            pltpu.VMEM((n, rows // 8, cw), bf16),
+            pltpu.VMEM((n, 2, seat, half), bf16),
+            pltpu.VMEM((n, 2, seat, half), bf16),
+            pltpu.VMEM((n, 2, 2, seat, half), bf16),
+            pltpu.VMEM((n, 2, 2, seat, half), bf16),
+            pltpu.VMEM((n, 2, seat, cw), bf16),
+            pltpu.VMEM((n, 2, seat, cw), bf16),
+            pltpu.VMEM((n, 2, seat, cw), bf16),
+            pltpu.VMEM((n, 2, seat, cw), bf16),
             dma((n,)),
             dma((n, 2)),
             dma((n, 2)),
             dma((n, 2, 2)),
             dma((n, 2, 2)),
-            dma((n,)),
-            dma((n,)),
+            dma((n, 2)),
+            dma((n, 2)),
+            dma((n, 2)),
+            dma((n, 2)),
         ],
         compiler_params=pltpu.CompilerParams(
-            collective_id=1, has_side_effects=True, vmem_limit_bytes=48 * MIB
+            collective_id=1, has_side_effects=True, vmem_limit_bytes=60 * MIB
         ),
         name="project_out",
     )(attended, w_out)
@@ -644,7 +667,7 @@
             dma((PARTS, 16)),
         ],
         compiler_params=pltpu.CompilerParams(
-            collective_id=2, has_side_effects=True, vmem_limit_bytes=48 * MIB
+            collective_id=2, has_side_effects=True, vmem_limit_bytes=60 * MIB
         ),
         name="gather_and_project",
     )(node_target.reshape(1, rows), node_rows, cosine, sine, w_query, w_key, w_value)

time: 140 us -> 132 us (0.943)
  local copies, waits for them, and re-layouts: 7.31 us -> 1.87 us
  Pallas kernels: 129 us -> 125 us
    pallas_call x1, Pallas kernels: 46.3 us -> 38.6 us  [project_out(): pl.pallas_call(project_out_kernel, out_shape=jax.ShapeDtypeStruct((seat,...]
    unnamed x15 -> x1, local copies, waits for them, and re-layouts: 7.31 us -> 1.87 us
    pallas_call x1, Pallas kernels: 7.89 us -> 10.5 us  [attend(): pl.pallas_call(attend_kernel, out_shape=jax.ShapeDtypeStruct(queries.shap...]
where the time goes in v5:
time: 132 us; the launch traced here: 130 us
  Pallas kernels  125 us (95%)
  other arithmetic  2.68 us (2%)
  local copies, waits for them, and re-layouts  1.87 us (1%)
    pallas_call x1, Pallas kernels, gather_and_project(): pl.pallas_call(gather_kernel, out_shape=(jax.ShapeDtypeStruct((rows, 512)...  76 us
    pallas_call x1, Pallas kernels, project_out(): pl.pallas_call(project_out_kernel, out_shape=jax.ShapeDtypeStruct((seat,...  38.6 us
    pallas_call x1, Pallas kernels, attend(): pl.pallas_call(attend_kernel, out_shape=jax.ShapeDtypeStruct(queries.shap...  10.5 us

profile of v5, /device:TPU:34, one launch (start us, length us, event | category | flops | bytes accessed | tf_op | source)
XLA Modules:
  0.0 129.8 jit_solution(7690175078534242562)
XLA Ops:
  0.0 0.7 convert_element_type.3
  0.7 1.0 fusion
  1.7 1.0 pad_maximum_fusion
  2.7 76.0 %gather_and_project.1 = (bf16[512,512]{1,0:T(8,128)(2,1)}, bf16[8192,256]{1,0:T(8,128)(2,1)}) custom-call(s32[1,512]{1,0:T(1,128)} %bitcast.1, bf16[512,512]{1,0:T(8,128)(2,1)} %x_hbm.1, f32[512,128]{1,0:T(8,128)} %get-tuple-element.12.cos_hbm, f32[512,128]{1,0:T(8,128)} %get-tuple-element.13.sin_hbm, bf16[4096,512]{1,0:T(8,128)(2,1)} %wq_hbm.1, ...), custom_call_target="tpu_custom_call" | custom-call | tf_op jit(solution)/shard_map/gather_and_project/pallas_call | solution.py:636
  78.7 10.5 %attend.1.att_ref = bf16[512,512]{1,0:T(8,128)(2,1)} custom-call(s32[4,64]{1,0:T(4,128)} %mask_ref.1, bf16[512,512]{1,0:T(8,128)(2,1)} %get-tuple-element.7.q_ref, bf16[8192,256]{1,0:T(8,128)(2,1)} %get-tuple-element.8.kv_ref), custom_call_target="tpu_custom_call" | custom-call | tf_op jit(solution)/shard_map/attend/pallas_call | solution.py:111
  89.2 38.6 %project_out.1 = bf16[64,4096]{1,0:T(8,128)(2,1)} custom-call(bf16[512,512]{1,0:T(8,128)(2,1)} %attend.1.att_ref, bf16[512,4096]{1,0:T(8,128)(2,1)} %w_hbm.1), custom_call_target="tpu_custom_call" | custom-call | tf_op jit(solution)/shard_map/project_out/pallas_call | solution.py:288
  127.9 1.9 %copy.10 = bf16[64,4096]{1,0:T(8,128)(2,1)} copy(bf16[64,4096]{1,0:T(8,128)(2,1)} %project_out.1) | data formatting | bytes 1048576
  (1 shorter events, 0.0 us)

commit v6 on v5

--- a/solution.py
+++ b/solution.py
@@ -25,101 +25,113 @@
     return jnp.concatenate([cosine, cosine], axis=-1), jnp.concatenate([-sine, sine], axis=-1)
 
 
-def attend_kernel(mask_ref, q_ref, kv_ref, out_ref, list_ref, acc_ref):
+def attend_kernel(mask_ref, q_ref, kv_hbm, out_ref, list_ref, kv_ref, own_ref, acc_ref, stat_ref, sem):
     ctx = lax.axis_index("ctx")
-    local_blocks = q_ref.shape[0] // BLOCK
+    rows = q_ref.shape[0]
+    local_blocks = rows // BLOCK
     heads = q_ref.shape[1] // HD
     block_count = mask_ref.shape[1]
     width = heads * BLOCK
-    scale = 1.0 / math.sqrt(HD)
-
+    scale = math.log2(math.e) / math.sqrt(HD)
+    own = pl.ds(pl.multiple_of(ctx * rows, BLOCK), rows)
+    own_load = pltpu.make_async_copy(kv_hbm.at[own], own_ref, sem.at[0])
+    load = pltpu.make_async_copy(kv_hbm, kv_ref, sem.at[1])
+    own_load.start()
+    load.start()
+
+    def build(kb, counts):
+        for b in range(local_blocks):
+            list_ref[b, counts[b]] = kb
+        return tuple(n + mask_ref[b, kb] for b, n in enumerate(counts))
+
+    counts = lax.fori_loop(
+        0, block_count, build, (jnp.int32(0),) * local_blocks, unroll=8
+    )
+
+    def queries_of(b):
+        at = slice(b * BLOCK, (b + 1) * BLOCK)
+        return jnp.concatenate([q_ref[at, h * HD : (h + 1) * HD] for h in range(heads)], axis=0)
+
+    def score(keys, b):
+        return scale * lax.dot_general(
+            keys, queries_of(b), (((1,), (1,)), ((), ())), preferred_element_type=jnp.float32
+        )
+
+    def mix(values, weights):
+        return lax.dot_general(
+            values, weights.astype(jnp.bfloat16), (((0,), (0,)), ((), ())),
+            preferred_element_type=jnp.float32,
+        )
+
+    own_load.wait()
+    key_at = lax.broadcasted_iota(jnp.int32, (BLOCK, width), 0)
+    query_at = lax.broadcasted_iota(jnp.int32, (BLOCK, width), 1) % BLOCK
     for b in range(local_blocks):
-        qb = ctx * local_blocks + b
-
-        def build(kb, n):
-            list_ref[n] = kb
-            return n + jnp.where(kb < qb, mask_ref[b, kb], 0)
-
-        count = lax.fori_loop(0, block_count, build, 0, unroll=8)
-        list_ref[count] = 0
-        rows = pl.ds(b * BLOCK, BLOCK)
-        queries = jnp.concatenate(
-            [q_ref[rows, h * HD : (h + 1) * HD] for h in range(heads)], axis=0
-        )
-
-        def scores_of(kb):
-            keys = kv_ref[pl.ds(pl.multiple_of(kb * BLOCK, BLOCK), BLOCK), 0:HD]
-            return (
-                lax.dot_general(
-                    keys, queries, (((1,), (1,)), ((), ())), preferred_element_type=jnp.float32
-                )
-                * scale
-            )
-
-        def mix(kb, weights):
-            values = kv_ref[pl.ds(pl.multiple_of(kb * BLOCK, BLOCK), BLOCK), HD : 2 * HD]
-            return lax.dot_general(
-                values,
-                weights.astype(jnp.bfloat16),
-                (((0,), (0,)), ((), ())),
-                preferred_element_type=jnp.float32,
-            )
-
-        key_at = lax.broadcasted_iota(jnp.int32, (BLOCK, width), 0)
-        query_at = lax.broadcasted_iota(jnp.int32, (BLOCK, width), 1) % BLOCK
-        scores = jnp.where(key_at <= query_at, scores_of(qb), NEG_LARGE)
+        at = slice(b * BLOCK, (b + 1) * BLOCK)
+        scores = jnp.where(key_at <= query_at, score(own_ref[at, 0:HD], b), NEG_LARGE)
         highest = jnp.max(scores, axis=0, keepdims=True)
-        weights = jnp.exp(scores - highest)
-        total = jnp.sum(weights, axis=0, keepdims=True)
-        acc_ref[...] = mix(qb, weights)
-
-        def step(i, state):
-            highest, total = state
-            first = list_ref[2 * i]
-            second = list_ref[2 * i + 1]
-            has_second = 2 * i + 1 < count
-            second = jnp.where(has_second, second, 0)
-            drop = jnp.where(has_second, 0.0, NEG_LARGE).astype(jnp.float32)
-            scores0 = scores_of(first)
-            scores1 = scores_of(second) + drop
-            new_highest = jnp.maximum(
-                highest,
-                jnp.maximum(
-                    jnp.max(scores0, axis=0, keepdims=True), jnp.max(scores1, axis=0, keepdims=True)
-                ),
-            )
-            factor = jnp.exp(highest - new_highest)
-            weights0 = jnp.exp(scores0 - new_highest)
-            weights1 = jnp.exp(scores1 - new_highest)
-            total = (
-                total * factor
-                + jnp.sum(weights0, axis=0, keepdims=True)
-                + jnp.sum(weights1, axis=0, keepdims=True)
-            )
-            acc_ref[...] = acc_ref[...] * factor + mix(first, weights0) + mix(second, weights1)
-            return new_highest, total
-
-        highest, total = lax.fori_loop(0, (count + 1) // 2, step, (highest, total))
-        attended = acc_ref[...] / total
+        weights = jnp.exp2(scores - highest)
+        stat_ref[b, 0:1] = highest
+        stat_ref[b, 1:2] = jnp.sum(weights, axis=0, keepdims=True)
+        acc_ref[b] = mix(own_ref[at, HD : 2 * HD], weights)
+    load.wait()
+
+    def add_two(b, i):
+        places, drops = [], []
+        for at in (2 * i, 2 * i + 1):
+            real = at < counts[b]
+            kb = jnp.where(real, list_ref[b, jnp.where(real, at, 0)], 0)
+            places.append(pl.ds(pl.multiple_of(kb * BLOCK, BLOCK), BLOCK))
+            drops.append(jnp.where(real, 0.0, NEG_LARGE).astype(jnp.float32))
+        keys = jnp.concatenate([kv_ref[at, 0:HD] for at in places], axis=0)
+        values = jnp.concatenate([kv_ref[at, HD : 2 * HD] for at in places], axis=0)
+        scores = score(keys, b)
+        scores = jnp.concatenate(
+            [scores[:BLOCK] + drops[0], scores[BLOCK:] + drops[1]], axis=0
+        )
+        old = stat_ref[b, 0:1]
+        highest = jnp.maximum(old, jnp.max(scores, axis=0, keepdims=True))
+        factor = jnp.exp2(old - highest)
+        weights = jnp.exp2(scores - highest)
+        stat_ref[b, 0:1] = highest
+        stat_ref[b, 1:2] = stat_ref[b, 1:2] * factor + jnp.sum(weights, axis=0, keepdims=True)
+        acc_ref[b] = acc_ref[b] * factor + mix(values, weights)
+
+    for b in range(0, local_blocks, 2):
+
+        def step(i, carry, b=b):
+            add_two(b, i)
+            add_two(b + 1, i)
+            return carry
+
+        lax.fori_loop(0, (jnp.maximum(counts[b], counts[b + 1]) + 1) // 2, step, 0)
+    for b in range(local_blocks):
+        attended = acc_ref[b] / stat_ref[b, 1:2]
         for h in range(heads):
-            out_ref[rows, h * HD : (h + 1) * HD] = attended[
+            out_ref[b * BLOCK : (b + 1) * BLOCK, h * HD : (h + 1) * HD] = attended[
                 :, h * BLOCK : (h + 1) * BLOCK
             ].T.astype(jnp.bfloat16)
 
 
 def attend(block_mask, queries, kv):
+    rows, width = queries.shape
+    blocks = rows // BLOCK
     return pl.pallas_call(
         attend_kernel,
         out_shape=jax.ShapeDtypeStruct(queries.shape, jnp.bfloat16),
         in_specs=[
             pl.BlockSpec(memory_space=pltpu.SMEM),
             pl.BlockSpec(memory_space=pltpu.VMEM),
-            pl.BlockSpec(memory_space=pltpu.VMEM),
+            pl.BlockSpec(memory_space=pltpu.HBM),
         ],
         out_specs=pl.BlockSpec(memory_space=pltpu.VMEM),
         scratch_shapes=[
-            pltpu.SMEM((128,), jnp.int32),
-            pltpu.VMEM((HD, queries.shape[1]), jnp.float32),
+            pltpu.SMEM((blocks, 128), jnp.int32),
+            pltpu.VMEM(kv.shape, jnp.bfloat16),
+            pltpu.VMEM((rows, kv.shape[1]), jnp.bfloat16),
+            pltpu.VMEM((blocks, HD, width), jnp.float32),
+            pltpu.VMEM((blocks, 8, width), jnp.float32),
+            pltpu.SemaphoreType.DMA((2,)),
         ],
         compiler_params=pltpu.CompilerParams(vmem_limit_bytes=60 * MIB),
         name="attend",
@@ -161,8 +173,7 @@
         pltpu.make_async_copy(w_hbm.at[:, pl.ds(c * cw, cw)], w_ref.at[c], w_sem.at[c])
         for c in range(OUT_CHUNKS)
     ]
-    for load in loads:
-        load.start()
+    loads[0].start()
     barrier = pltpu.get_barrier_semaphore()
     for peer in (up, down, across):
         pl.semaphore_signal(
@@ -204,6 +215,9 @@
 
     def first(c):
         loads[c].wait()
+        if c == 0:
+            for load in loads[1:]:
+                load.start()
         part[c] = jnp.dot(att_ref[...], w_ref[c], preferred_element_type=f32)
         if c == 0:
             pl.semaphore_wait(barrier, 3)
@@ -315,27 +329,33 @@
             dma((n, 2)),
         ],
         compiler_params=pltpu.CompilerParams(
-            collective_id=1, has_side_effects=True, vmem_limit_bytes=60 * MIB
+            collective_id=1, has_side_effects=True, vmem_limit_bytes=56 * MIB
         ),
         name="project_out",
     )(attended, w_out)
 
 
-IN_CHUNKS = 4
-PARTS = 2
+IN_CHUNKS = 2
+PART_ROWS = (256, 256)
+PART_CHUNKS = (2, 1)
 SLOTS = 64
+AHEAD = 3
+QUERIES_LATER = 0
+STEPS = [(p, f) for p, n in enumerate(PART_CHUNKS) for f in range(n)]
+PARTS = len(PART_ROWS)
 
 
 def gather_kernel(
     target_ref, x_hbm, cos_hbm, sin_hbm, wq_hbm, wk_hbm, wv_hbm, q_ref, kv_ref,
-    x_ref, cos_ref, sin_ref, w_ref, pick, place, send, recv, meta_out, meta_in, pieces, acc,
-    kv_own, in_sem, row_ss, row_rs, meta_ss, meta_rs, ag_ss, ag_rs, kv_sem, kv_ss, kv_rs,
+    x_ref, cos_ref, sin_ref, w_ref, pick, place, send, recv, meta_out, meta_in, in_sem, row_ss,
+    row_rs, meta_ss, meta_rs, ag_ss, ag_rs, kv_sem, kv_ss, kv_rs, *per_part,
 ):
     ctx = lax.axis_index("ctx")
     peers = lax.axis_size("ctx")
     rows, cols = x_ref.shape
     chunk = cols // IN_CHUNKS
-    part_rows = rows // PARTS
+    pieces, acc, kv_own = (per_part[i * PARTS : (i + 1) * PARTS] for i in range(3))
+    starts = [sum(PART_ROWS[:p]) for p in range(PARTS)]
     y, zh, up, down, across = ring_places()
     bf16 = jnp.bfloat16
     loads = [
@@ -351,8 +371,7 @@
             )
         )
     ]
-    for load in loads:
-        load.start()
+    loads[0].start()
     barrier = pltpu.get_barrier_semaphore()
     for k in range(1, peers):
         pl.semaphore_signal(
@@ -396,33 +415,34 @@
             row_ss.at[f, k], row_rs.at[f, k], ctx=to,
         )
 
+    line = lax.broadcasted_iota(jnp.int32, (8, rows), 0)
+    high = local // 16
+    facts = jnp.where(line == 0, high, jnp.where(line == 1, local - high * 16, 1))
+    facts = lax.dot_general(
+        facts.astype(jnp.float32).astype(bf16), pick[...], (((1,), (1,)), ((), ())),
+        preferred_element_type=jnp.float32,
+    )
+    goes_to = jnp.where(facts[2:3] > 0.5, facts[0:1] * 16.0 + facts[1:2], -1.0)
+    goes_to = jnp.broadcast_to(goes_to, (8, peers * SLOTS))
+    for i in range(peers // 2):
+        tile = goes_to[:, i * 128 : (i + 1) * 128]
+        meta_out[2 * i] = tile
+        meta_out[2 * i + 1] = pltpu.roll(tile, SLOTS, 1)
+    pl.semaphore_wait(barrier, peers - 1 + 3)
+    for k in range(1, peers):
+        meta_copy(k).start()
+    meta_in[0] = meta_out[ctx]
+
     loads[0].wait()
+    for load in loads[1:]:
+        load.start()
     for f in range(IN_CHUNKS):
         send[f] = jnp.dot(
             pick[...], x_ref[:, f * chunk : (f + 1) * chunk], preferred_element_type=jnp.float32
         ).astype(bf16)
-        if f == 0:
-            pl.semaphore_wait(barrier, peers - 1 + 3)
         for k in range(1, peers):
             row_copy(f, k).start()
         recv[f, 0:SLOTS, :] = send[f, pl.ds(pl.multiple_of(ctx * SLOTS, SLOTS), SLOTS), :]
-        if f == 0:
-            line = lax.broadcasted_iota(jnp.int32, (8, rows), 0)
-            high = local // 16
-            facts = jnp.where(line == 0, high, jnp.where(line == 1, local - high * 16, 1))
-            facts = lax.dot_general(
-                facts.astype(jnp.float32).astype(bf16), pick[...], (((1,), (1,)), ((), ())),
-                preferred_element_type=jnp.float32,
-            )
-            goes_to = jnp.where(facts[2:3] > 0.5, facts[0:1] * 16.0 + facts[1:2], -1.0)
-            goes_to = jnp.broadcast_to(goes_to, (8, peers * SLOTS))
-            for i in range(peers // 2):
-                tile = goes_to[:, i * 128 : (i + 1) * 128]
-                meta_out[2 * i] = tile
-                meta_out[2 * i + 1] = pltpu.roll(tile, SLOTS, 1)
-            for k in range(1, peers):
-                meta_copy(k).start()
-            meta_in[0] = meta_out[ctx]
 
     for k in range(1, peers):
         meta_copy(k).wait_recv()
@@ -433,46 +453,51 @@
         at = lax.broadcasted_iota(jnp.int32, (rows, 128), 0)
         place[:, i * 128 : (i + 1) * 128] = jnp.where(at == both, 1.0, 0.0).astype(bf16)
 
-    half = part_rows // 2
-
     def piece(dy, other):
         return ((y + dy) % 4) * 2 + ((1 - zh) if other else zh)
 
     def spread(n, e):
-        part, f = divmod(n, IN_CHUNKS)
+        part, f = STEPS[n]
+        size, half = PART_ROWS[part], PART_ROWS[part] // 2
         src, lo, size, to = (
-            (piece(0, 0), 0, part_rows, across),
-            (piece(0, 0), 0, part_rows, up),
-            (piece(0, 0), 0, part_rows, down),
+            (piece(0, 0), 0, size, across),
+            (piece(0, 0), 0, size, up),
+            (piece(0, 0), 0, size, down),
             (piece(3, 0), 0, half, up),
             (piece(1, 0), half, half, down),
-            (piece(0, 1), 0, part_rows, up),
-            (piece(0, 1), 0, part_rows, down),
-            (piece(2, 0), 0, part_rows, across),
+            (piece(0, 1), 0, size, up),
+            (piece(0, 1), 0, size, down),
+            (piece(2, 0), 0, size, across),
         )[e]
-        ref = pieces.at[src, part, f, pl.ds(lo, size)]
+        ref = pieces[part].at[src, f, pl.ds(lo, size)]
         return remote(ref, ref, ag_ss.at[n, e], ag_rs.at[n, e], head=to)
 
+    def product(part, index, columns):
+        piece_rows = jnp.concatenate(
+            [pieces[part][index, g] for g in range(PART_CHUNKS[part])], axis=1
+        )
+        deep = index * cols
+        deep = pl.ds(deep if isinstance(deep, int) else pl.multiple_of(deep, cols), cols)
+        return jnp.dot(piece_rows, w_ref[deep, columns], preferred_element_type=jnp.float32)
+
     def project(n, index, first=False):
-        part, f = divmod(n, IN_CHUNKS)
-        if f < IN_CHUNKS - 1:
+        part, f = STEPS[n]
+        if f < PART_CHUNKS[part] - 1:
             return
-        piece_rows = jnp.concatenate(
-            [pieces[index, part, g] for g in range(IN_CHUNKS)], axis=1
-        )
-        deep = pl.ds(pl.multiple_of(index * cols, cols), cols)
-        term = jnp.dot(piece_rows, w_ref[deep, :], preferred_element_type=jnp.float32)
-        acc[part] = term if first else acc[part] + term
+        term = product(part, index, slice(512, 768))
+        acc[part][...] = term if first else acc[part][...] + term
 
     def begin(n):
-        part, f = divmod(n, IN_CHUNKS)
+        part, f = STEPS[n]
         if part == 0:
             for k in range(1, peers):
                 row_copy(f, k).wait_recv()
-        here = slice(part * part_rows, (part + 1) * part_rows)
-        pieces[piece(0, 0), part, f] = jnp.dot(
-            place[here, :], recv[f], preferred_element_type=jnp.float32
-        ).astype(bf16)
+        here = slice(starts[part], starts[part] + PART_ROWS[part])
+        wide = IN_CHUNKS // PART_CHUNKS[part]
+        for g in range(wide):
+            pieces[part][piece(0, 0), f, :, g * chunk : (g + 1) * chunk] = jnp.dot(
+                place[here, :], recv[f * wide + g], preferred_element_type=jnp.float32
+            ).astype(bf16)
         for e in (1, 2, 0):
             spread(n, e).start()
         if n == IN_CHUNKS - 1:
@@ -507,7 +532,6 @@
         project(n, piece(2, 1))
 
     zl, x, core = ctx // 8, (ctx // 2) % 4, ctx % 2
-    kv_half = part_rows // 2
 
     def block(dx, other_z, other_core=0):
         z = (1 - zl) if other_z else zl
@@ -518,6 +542,7 @@
 
     def share(part, e):
         right, left, over = block(1, 0), block(3, 0), block(0, 1)
+        part_rows, kv_half = PART_ROWS[part], PART_ROWS[part] // 2
         if e >= 8:
             src, lo, size, to = block(*kv_pieces[e - 8]), 0, part_rows, block(0, 0, 1)
         else:
@@ -532,31 +557,34 @@
                 (block(2, 0), 0, part_rows, over),
             )[e]
         ref = kv_ref.at[
-            pl.ds(pl.multiple_of(src * rows + part * part_rows + lo, 16), size)
+            pl.ds(pl.multiple_of(src * rows + starts[part] + lo, 16), size)
         ]
-        source = kv_own.at[part] if e in (0, 1, 2, 8) else ref
+        source = kv_own[part] if e in (0, 1, 2, 8) else ref
         return remote(source, ref, kv_ss.at[part, e], kv_rs.at[part, e], ctx=to)
 
     def keep(part):
-        at = pl.ds(pl.multiple_of(ctx * rows + part * part_rows, 16), part_rows)
-        return pltpu.make_async_copy(kv_own.at[part], kv_ref.at[at], kv_sem.at[part])
+        at = pl.ds(pl.multiple_of(ctx * rows + starts[part], 16), PART_ROWS[part])
+        return pltpu.make_async_copy(kv_own[part], kv_ref.at[at], kv_sem.at[part])
+
+    def turn(tensor, here):
+        return tensor * cos_ref[here, :] + pltpu.roll(tensor, HD // 2, 1) * sin_ref[here, :]
 
     def finish(part):
-        here = slice(part * part_rows, (part + 1) * part_rows)
-        cosine, sine = cos_ref[here, :], sin_ref[here, :]
-        for h in (4, 5, 0, 1, 2, 3):
-            tensor = acc[part, :, h * HD : (h + 1) * HD]
-            if h < 5:
-                tensor = tensor * cosine + pltpu.roll(tensor, HD // 2, 1) * sine
-            tensor = tensor.astype(bf16)
-            if h < 4:
-                q_ref[here, h * HD : (h + 1) * HD] = tensor
-            else:
-                kv_own[part, :, (h - 4) * HD : (h - 3) * HD] = tensor
-            if h == 5:
-                for e in (1, 2, 0, 8):
-                    share(part, e).start()
-                keep(part).start()
+        here = slice(starts[part], starts[part] + PART_ROWS[part])
+        kv_own[part][:, 0:HD] = turn(acc[part][:, 0:HD], here).astype(bf16)
+        kv_own[part][:, HD : 2 * HD] = acc[part][:, HD : 2 * HD].astype(bf16)
+        for e in (1, 2, 0, 8):
+            share(part, e).start()
+        keep(part).start()
+
+    def finish_queries(part):
+        here = slice(starts[part], starts[part] + PART_ROWS[part])
+        query = product(part, 0, slice(0, 512))
+        for index in range(1, 8):
+            query = query + product(part, index, slice(0, 512))
+        for h in range(4):
+            at = slice(h * HD, (h + 1) * HD)
+            q_ref[here, at] = turn(query[:, at], here).astype(bf16)
 
     def share_near(part):
         share(part, 1).wait_recv()
@@ -584,29 +612,30 @@
         share(part, 7).wait_recv()
         share(part, 15).start()
 
-    count = IN_CHUNKS * PARTS
+    count = len(STEPS)
+    due = {}
+    for part in range(PARTS):
+        last = sum(PART_CHUNKS[: part + 1]) + 1
+        for later, rank_in, act in (
+            (0, 0, finish), (1, 1, share_near), (2, 1, share_far), (3, 1, share_other),
+            (QUERIES_LATER, 2, finish_queries),
+        ):
+            due.setdefault(last + later, []).append((rank_in, part, act))
     begin(0)
     begin(1)
-    for n in range(count + 2):
+    begun = 2
+    for n in range(max(due) + 1):
         if n < count:
             near(n)
-        if n + 2 < count:
-            begin(n + 2)
+        while begun < min(count, n + (3 if n + 3 <= IN_CHUNKS - 1 or n < 1 else AHEAD + 1)):
+            begin(begun)
+            begun += 1
         if 1 <= n <= count:
             far(n - 1)
-        if n >= 2:
+        if 2 <= n <= count + 1:
             other(n - 2)
-        if n == IN_CHUNKS + 1:
-            finish(0)
-        if n == IN_CHUNKS + 2:
-            share_near(0)
-        if n == IN_CHUNKS + 3:
-            share_far(0)
-    finish(1)
-    share_other(0)
-    share_near(1)
-    share_far(1)
-    share_other(1)
+        for rank_in, part, act in sorted(due.get(n, []), key=lambda item: item[:2]):
+            act(part)
     for part in range(PARTS):
         for e in range(8, 16):
             share(part, e).wait_recv()
@@ -628,7 +657,6 @@
     rows, cols = node_rows.shape
     peers = lax.axis_size("ctx")
     chunk = cols // IN_CHUNKS
-    part_rows = rows // PARTS
     bf16 = jnp.bfloat16
     dma = pltpu.SemaphoreType.DMA
     vmem = pl.BlockSpec(memory_space=pltpu.VMEM)
@@ -652,20 +680,20 @@
             pltpu.VMEM((IN_CHUNKS, peers * SLOTS, chunk), bf16),
             pltpu.VMEM((peers, 8, 128), jnp.float32),
             pltpu.VMEM((peers, 8, 128), jnp.float32),
-            pltpu.VMEM((8, PARTS, IN_CHUNKS, part_rows, chunk), bf16),
-            pltpu.VMEM((PARTS, part_rows, 768), jnp.float32),
-            pltpu.VMEM((PARTS, part_rows, 256), bf16),
             dma((6,)),
             dma((IN_CHUNKS, peers)),
             dma((IN_CHUNKS, peers)),
             dma((peers,)),
             dma((peers,)),
-            dma((PARTS * IN_CHUNKS, 8)),
-            dma((PARTS * IN_CHUNKS, 8)),
+            dma((len(STEPS), 8)),
+            dma((len(STEPS), 8)),
             dma((PARTS,)),
             dma((PARTS, 16)),
             dma((PARTS, 16)),
-        ],
+        ]
+        + [pltpu.VMEM((8, n, r, cols // n), bf16) for r, n in zip(PART_ROWS, PART_CHUNKS)]
+        + [pltpu.VMEM((r, 256), jnp.float32) for r in PART_ROWS]
+        + [pltpu.VMEM((r, 256), bf16) for r in PART_ROWS],
         compiler_params=pltpu.CompilerParams(
             collective_id=2, has_side_effects=True, vmem_limit_bytes=60 * MIB
         ),

time: 132 us -> 127 us (0.962); the launches traced: 130 us -> 126 us
  Pallas kernels: 125 us -> 122 us
    pallas_call x1, Pallas kernels: 76 us -> 73.1 us  [gather_and_project(): pl.pallas_call(gather_kernel, out_shape=(jax.ShapeDtypeStruct((rows, 512)...]
where the time goes in v6:
time: 127 us; the launch traced here: 126 us
  Pallas kernels  122 us (96%)
  other arithmetic  2.68 us (2%)
  local copies, waits for them, and re-layouts  1.87 us (1%)
    pallas_call x1, Pallas kernels, gather_and_project(): pl.pallas_call(gather_kernel, out_shape=(jax.ShapeDtypeStruct((rows, 512)...  73.1 us
    pallas_call x1, Pallas kernels, project_out(): pl.pallas_call(project_out_kernel, out_shape=jax.ShapeDtypeStruct((seat,...  38.4 us
    pallas_call x1, Pallas kernels, attend(): pl.pallas_call(attend_kernel, out_shape=jax.ShapeDtypeStruct(queries.shap...  10.2 us

profile of v6, /device:TPU:34, one launch (start us, length us, event | category | flops | bytes accessed | tf_op | source)
XLA Modules:
  0.0 126.4 jit_solution(14114531340047653572)
XLA Ops:
  0.0 0.7 convert_element_type.3
  0.7 1.0 fusion
  1.7 1.0 pad_maximum_fusion
  2.7 73.1 %gather_and_project.1 = (bf16[512,512]{1,0:T(8,128)(2,1)}, bf16[8192,256]{1,0:T(8,128)(2,1)}) custom-call(s32[1,512]{1,0:T(1,128)} %bitcast.1, bf16[512,512]{1,0:T(8,128)(2,1)} %x_hbm.1, f32[512,128]{1,0:T(8,128)} %get-tuple-element.12.cos_hbm, f32[512,128]{1,0:T(8,128)} %get-tuple-element.13.sin_hbm, bf16[4096,512]{1,0:T(8,128)(2,1)} %wq_hbm.1, ...), custom_call_target="tpu_custom_call" | custom-call | tf_op jit(solution)/shard_map/gather_and_project/pallas_call | solution.py:664
  75.8 10.2 %attend.1.att_ref = bf16[512,512]{1,0:T(8,128)(2,1)} custom-call(s32[4,64]{1,0:T(4,128)} %mask_ref.1, bf16[512,512]{1,0:T(8,128)(2,1)} %get-tuple-element.7.q_ref, bf16[8192,256]{1,0:T(8,128)(2,1)} %get-tuple-element.8.kv_hbm), custom_call_target="tpu_custom_call" | custom-call | tf_op jit(solution)/shard_map/attend/pallas_call | solution.py:119
  86.1 38.4 %project_out.1 = bf16[64,4096]{1,0:T(8,128)(2,1)} custom-call(bf16[512,512]{1,0:T(8,128)(2,1)} %attend.1.att_ref, bf16[512,4096]{1,0:T(8,128)(2,1)} %w_hbm.1), custom_call_target="tpu_custom_call" | custom-call | tf_op jit(solution)/shard_map/project_out/pallas_call | solution.py:302
  124.5 1.9 %copy.10 = bf16[64,4096]{1,0:T(8,128)(2,1)} copy(bf16[64,4096]{1,0:T(8,128)(2,1)} %project_out.1) | data formatting | bytes 1048576
  (1 shorter events, 0.0 us)

commit v7 on v6

--- a/solution.py
+++ b/solution.py
@@ -2,6 +2,7 @@
 
 import jax
 import jax.numpy as jnp
+import numpy as np
 from jax import lax
 from jax.experimental import pallas as pl
 from jax.experimental.pallas import tpu as pltpu
@@ -12,17 +13,6 @@
 ROPE_THETA = 500000.0
 NEG_LARGE = -1e30
 MIB = 1024 * 1024
-
-
-def rotary_tables(positions, head_size):
-    half_size = head_size // 2
-    inverse = jnp.exp(
-        jnp.arange(half_size, dtype=jnp.float32) * (-2.0 * math.log(ROPE_THETA) / head_size)
-    )
-    angles = positions.astype(jnp.float32)[:, None] * inverse[None, :]
-    cosine = jnp.cos(angles)
-    sine = jnp.sin(angles)
-    return jnp.concatenate([cosine, cosine], axis=-1), jnp.concatenate([-sine, sine], axis=-1)
 
 
 def attend_kernel(mask_ref, q_ref, kv_hbm, out_ref, list_ref, kv_ref, own_ref, acc_ref, stat_ref, sem):
@@ -106,11 +96,11 @@
 
         lax.fori_loop(0, (jnp.maximum(counts[b], counts[b + 1]) + 1) // 2, step, 0)
     for b in range(local_blocks):
-        attended = acc_ref[b] / stat_ref[b, 1:2]
+        attended = (acc_ref[b] * (1.0 / stat_ref[b, 1:2])).astype(jnp.bfloat16)
         for h in range(heads):
             out_ref[b * BLOCK : (b + 1) * BLOCK, h * HD : (h + 1) * HD] = attended[
                 :, h * BLOCK : (h + 1) * BLOCK
-            ].T.astype(jnp.bfloat16)
+            ].T
 
 
 def attend(block_mask, queries, kv):
@@ -336,8 +326,8 @@
 
 
 IN_CHUNKS = 2
-PART_ROWS = (256, 256)
-PART_CHUNKS = (2, 1)
+PART_ROWS = (256, 128, 128)
+PART_CHUNKS = (2, 1, 1)
 SLOTS = 64
 AHEAD = 3
 QUERIES_LATER = 0
@@ -346,7 +336,7 @@
 
 
 def gather_kernel(
-    target_ref, x_hbm, cos_hbm, sin_hbm, wq_hbm, wk_hbm, wv_hbm, q_ref, kv_ref,
+    target_ref, position_ref, turn_ref, x_hbm, wq_hbm, wk_hbm, wv_hbm, q_ref, kv_ref,
     x_ref, cos_ref, sin_ref, w_ref, pick, place, send, recv, meta_out, meta_in, in_sem, row_ss,
     row_rs, meta_ss, meta_rs, ag_ss, ag_rs, kv_sem, kv_ss, kv_rs, *per_part,
 ):
@@ -366,8 +356,6 @@
                 (wq_hbm, w_ref.at[:, 0:512]),
                 (wk_hbm, w_ref.at[:, 512:640]),
                 (wv_hbm, w_ref.at[:, 640:768]),
-                (cos_hbm, cos_ref),
-                (sin_hbm, sin_ref),
             )
         )
     ]
@@ -443,6 +431,13 @@
         for k in range(1, peers):
             row_copy(f, k).start()
         recv[f, 0:SLOTS, :] = send[f, pl.ds(pl.multiple_of(ctx * SLOTS, SLOTS), SLOTS), :]
+
+    for i in range(rows // 128):
+        here = slice(i * 128, (i + 1) * 128)
+        angle = position_ref[:, here].astype(jnp.float32)
+        angle = jnp.broadcast_to(angle, (128, 128)).T * turn_ref[0:1]
+        cos_ref[here, :] = jnp.cos(angle)
+        sin_ref[here, :] = jnp.sin(angle) * turn_ref[1:2]
 
     for k in range(1, peers):
         meta_copy(k).wait_recv()
@@ -542,24 +537,21 @@
 
     def share(part, e):
         right, left, over = block(1, 0), block(3, 0), block(0, 1)
-        part_rows, kv_half = PART_ROWS[part], PART_ROWS[part] // 2
+        part_rows = PART_ROWS[part]
         if e >= 8:
-            src, lo, size, to = block(*kv_pieces[e - 8]), 0, part_rows, block(0, 0, 1)
+            src, to = block(*kv_pieces[e - 8]), block(0, 0, 1)
         else:
-            src, lo, size, to = (
-                (block(0, 0), 0, part_rows, over),
-                (block(0, 0), 0, part_rows, right),
-                (block(0, 0), 0, part_rows, left),
-                (block(3, 0), 0, kv_half, right),
-                (block(1, 0), kv_half, kv_half, left),
-                (block(0, 1), 0, part_rows, right),
-                (block(0, 1), 0, part_rows, left),
-                (block(2, 0), 0, part_rows, over),
+            src, to = (
+                (block(0, 0), over),
+                (block(0, 0), right),
+                (block(0, 0), left),
+                (block(0, 0), block(2, 0)),
+                (block(0, 1), right),
+                (block(0, 1), left),
+                (block(0, 1), block(2, 0)),
             )[e]
-        ref = kv_ref.at[
-            pl.ds(pl.multiple_of(src * rows + starts[part] + lo, 16), size)
-        ]
-        source = kv_own[part] if e in (0, 1, 2, 8) else ref
+        ref = kv_ref.at[pl.ds(pl.multiple_of(src * rows + starts[part], 16), part_rows)]
+        source = kv_own[part] if e in (0, 1, 2, 3, 8) else ref
         return remote(source, ref, kv_ss.at[part, e], kv_rs.at[part, e], ctx=to)
 
     def keep(part):
@@ -573,8 +565,11 @@
         here = slice(starts[part], starts[part] + PART_ROWS[part])
         kv_own[part][:, 0:HD] = turn(acc[part][:, 0:HD], here).astype(bf16)
         kv_own[part][:, HD : 2 * HD] = acc[part][:, HD : 2 * HD].astype(bf16)
-        for e in (1, 2, 0, 8):
-            share(part, e).start()
+        give(part, 0, zl == 0)
+        give(part, 1, x < 3)
+        give(part, 2, x == 0)
+        give(part, 3, x < 2)
+        share(part, 8).start()
         keep(part).start()
 
     def finish_queries(part):
@@ -586,31 +581,35 @@
             at = slice(h * HD, (h + 1) * HD)
             q_ref[here, at] = turn(query[:, at], here).astype(bf16)
 
+    def give(part, e, when):
+        @pl.when(when)
+        def _():
+            share(part, e).start()
+
     def share_near(part):
-        share(part, 1).wait_recv()
-        share(part, 3).start()
-        share(part, 10).start()
-        share(part, 2).wait_recv()
-        share(part, 4).start()
-        share(part, 11).start()
-        share(part, 0).wait_recv()
-        share(part, 5).start()
-        share(part, 6).start()
-        share(part, 9).start()
+        @pl.when(zl == 1)
+        def _():
+            share(part, 0).wait_recv()
+            for e in (4, 5, 6, 9):
+                share(part, e).start()
+
+    def pass_on(part, e, core_e, when):
+        @pl.when(when)
+        def _():
+            share(part, e).wait_recv()
+            share(part, core_e).start()
 
     def share_far(part):
-        share(part, 3).wait_recv()
-        share(part, 4).wait_recv()
-        share(part, 7).start()
-        share(part, 12).start()
+        pass_on(part, 1, 10, x > 0)
+        pass_on(part, 2, 11, x == 3)
+        pass_on(part, 3, 12, x > 1)
 
     def share_other(part):
-        share(part, 5).wait_recv()
-        share(part, 13).start()
-        share(part, 6).wait_recv()
-        share(part, 14).start()
-        share(part, 7).wait_recv()
-        share(part, 15).start()
+        @pl.when(zl == 1)
+        def _():
+            for e in (4, 5, 6):
+                share(part, e).wait_recv()
+                share(part, e + 9).start()
 
     count = len(STEPS)
     due = {}
@@ -636,9 +635,30 @@
             other(n - 2)
         for rank_in, part, act in sorted(due.get(n, []), key=lambda item: item[:2]):
             act(part)
+    below = zl == 1
+    sent = (
+        (0, zl == 0), (1, x < 3), (2, x == 0), (3, x < 2), (4, below), (5, below), (6, below),
+    )
+    copied = (
+        (8, None), (9, below), (10, x > 0), (11, x == 3), (12, x > 1), (13, below), (14, below),
+        (15, below),
+    )
+
+    def drain(part, e, when, received):
+        def wait():
+            if received:
+                share(part, e).wait_recv()
+            else:
+                share(part, e).wait_send()
+
+        if when is None:
+            wait()
+        else:
+            pl.when(when)(wait)
+
     for part in range(PARTS):
-        for e in range(8, 16):
-            share(part, e).wait_recv()
+        for e, when in copied:
+            drain(part, e, when, True)
 
     for k in range(1, peers):
         meta_copy(k).wait_send()
@@ -649,11 +669,11 @@
             spread(n, e).wait_send()
     for part in range(PARTS):
         keep(part).wait()
-        for e in range(16):
-            share(part, e).wait_send()
-
-
-def gather_and_project(node_rows, node_target, cosine, sine, w_query, w_key, w_value):
+        for e, when in sent + copied:
+            drain(part, e, when, False)
+
+
+def gather_and_project(node_rows, node_target, node_position, w_query, w_key, w_value):
     rows, cols = node_rows.shape
     peers = lax.axis_size("ctx")
     chunk = cols // IN_CHUNKS
@@ -661,13 +681,16 @@
     dma = pltpu.SemaphoreType.DMA
     vmem = pl.BlockSpec(memory_space=pltpu.VMEM)
     hbm = pl.BlockSpec(memory_space=pltpu.HBM)
+    entry = np.arange(HD)
+    inverse = ROPE_THETA ** ((entry % (HD // 2)) * (-2.0 / HD))
+    turns = np.stack([inverse, np.where(entry < HD // 2, -1.0, 1.0)]).astype(np.float32)
     return pl.pallas_call(
         gather_kernel,
         out_shape=(
             jax.ShapeDtypeStruct((rows, 512), bf16),
             jax.ShapeDtypeStruct((rows * peers, 256), bf16),
         ),
-        in_specs=[vmem] + [hbm] * 6,
+        in_specs=[vmem] * 3 + [hbm] * 4,
         out_specs=(vmem, hbm),
         scratch_shapes=[
             pltpu.VMEM((rows, cols), bf16),
@@ -680,7 +703,7 @@
             pltpu.VMEM((IN_CHUNKS, peers * SLOTS, chunk), bf16),
             pltpu.VMEM((peers, 8, 128), jnp.float32),
             pltpu.VMEM((peers, 8, 128), jnp.float32),
-            dma((6,)),
+            dma((4,)),
             dma((IN_CHUNKS, peers)),
             dma((IN_CHUNKS, peers)),
             dma((peers,)),
@@ -698,13 +721,15 @@
             collective_id=2, has_side_effects=True, vmem_limit_bytes=60 * MIB
         ),
         name="gather_and_project",
-    )(node_target.reshape(1, rows), node_rows, cosine, sine, w_query, w_key, w_value)
+    )(
+        node_target.reshape(1, rows), node_position.reshape(1, rows), jnp.asarray(turns), node_rows,
+        w_query, w_key, w_value,
+    )
 
 
 def on_device(node_rows, node_target, node_position, block_mask, w_query, w_key, w_value, w_out):
-    cosine, sine = rotary_tables(node_position, HD)
     queries, kv = gather_and_project(
-        node_rows, node_target, cosine, sine, w_query, w_key, w_value
+        node_rows, node_target, node_position, w_query, w_key, w_value
     )
     attended = attend(block_mask, queries, kv)
     return project_out(attended, w_out)

time: 127 us -> 123 us (0.969)
  other arithmetic: 2.68 us -> 0 us
  Pallas kernels: 122 us -> 120 us
    pallas_call x1, Pallas kernels: 38.4 us -> 41.2 us  [project_out(): pl.pallas_call(project_out_kernel, out_shape=jax.ShapeDtypeStruct((seat,...]
    pallas_call x1, Pallas kernels: 73.1 us -> 70.5 us  [gather_and_project(): pl.pallas_call(gather_kernel, out_shape=(jax.ShapeDtypeStruct((rows, 512)...]
    pallas_call x1, Pallas kernels: 10.2 us -> 8.57 us  [attend(): pl.pallas_call(attend_kernel, out_shape=jax.ShapeDtypeStruct(queries.shap...]
where the time goes in v7:
time: 123 us; the launch traced here: 122 us
  Pallas kernels  120 us (98%)
  local copies, waits for them, and re-layouts  1.87 us (2%)
    pallas_call x1, Pallas kernels, gather_and_project(): pl.pallas_call(gather_kernel, out_shape=(jax.ShapeDtypeStruct((rows, 512)...  70.5 us
    pallas_call x1, Pallas kernels, project_out(): pl.pallas_call(project_out_kernel, out_shape=jax.ShapeDtypeStruct((seat,...  41.2 us
    pallas_call x1, Pallas kernels, attend(): pl.pallas_call(attend_kernel, out_shape=jax.ShapeDtypeStruct(queries.shap...  8.57 us

profile of v7, /device:TPU:34, one launch (start us, length us, event | category | flops | bytes accessed | tf_op | source)
XLA Modules:
  0.0 122.1 jit_solution(11846380258966385921)
XLA Ops:
  0.0 70.5 %gather_and_project.1 = (bf16[512,512]{1,0:T(8,128)(2,1)}, bf16[8192,256]{1,0:T(8,128)(2,1)}) custom-call(s32[1,512]{1,0:T(1,128)} %bitcast.2, s32[1,512]{1,0:T(1,128)} %bitcast.3, f32[2,128]{1,0:T(2,128)} %constant.2.clone.turn_ref, bf16[512,512]{1,0:T(8,128)(2,1)} %x_hbm.1, bf16[4096,512]{1,0:T(8,128)(2,1)} %wq_hbm.1, bf16[4096,128]{1,0:T(8,128)(2,1)} %wk_hbm.1, ...), custom_call_target="tpu_custom_call" | custom-call | tf_op jit(solution)/shard_map/gather_and_project/pallas_call | solution.py:687
  70.5 8.6 %attend.1.att_ref = bf16[512,512]{1,0:T(8,128)(2,1)} custom-call(s32[4,64]{1,0:T(4,128)} %mask_ref.1, bf16[512,512]{1,0:T(8,128)(2,1)} %get-tuple-element.7.q_ref, bf16[8192,256]{1,0:T(8,128)(2,1)} %get-tuple-element.8.kv_hbm), custom_call_target="tpu_custom_call" | custom-call | tf_op jit(solution)/shard_map/attend/pallas_call | solution.py:109
  79.1 41.2 %project_out.1 = bf16[64,4096]{1,0:T(8,128)(2,1)} custom-call(bf16[512,512]{1,0:T(8,128)(2,1)} %attend.1.att_ref, bf16[512,4096]{1,0:T(8,128)(2,1)} %w_hbm.1), custom_call_target="tpu_custom_call" | custom-call | tf_op jit(solution)/shard_map/project_out/pallas_call | solution.py:292
  120.3 1.9 %copy.11 = bf16[64,4096]{1,0:T(8,128)(2,1)} copy(bf16[64,4096]{1,0:T(8,128)(2,1)} %project_out.1) | data formatting | bytes 1048576

commit v8 on v7

--- a/solution.py
+++ b/solution.py
@@ -108,7 +108,7 @@
     blocks = rows // BLOCK
     return pl.pallas_call(
         attend_kernel,
-        out_shape=jax.ShapeDtypeStruct(queries.shape, jnp.bfloat16),
+        out_shape=pltpu.VMEM(queries.shape, jnp.bfloat16),
         in_specs=[
             pl.BlockSpec(memory_space=pltpu.SMEM),
             pl.BlockSpec(memory_space=pltpu.VMEM),
@@ -291,7 +291,7 @@
     dma = pltpu.SemaphoreType.DMA
     return pl.pallas_call(
         project_out_kernel,
-        out_shape=jax.ShapeDtypeStruct((seat, width), bf16),
+        out_shape=pltpu.VMEM((seat, width), bf16),
         in_specs=[
             pl.BlockSpec(memory_space=pltpu.VMEM),
             pl.BlockSpec(memory_space=pltpu.HBM),
@@ -319,7 +319,7 @@
             dma((n, 2)),
         ],
         compiler_params=pltpu.CompilerParams(
-            collective_id=1, has_side_effects=True, vmem_limit_bytes=56 * MIB
+            collective_id=1, has_side_effects=True, vmem_limit_bytes=60 * MIB
         ),
         name="project_out",
     )(attended, w_out)
@@ -687,7 +687,7 @@
     return pl.pallas_call(
         gather_kernel,
         out_shape=(
-            jax.ShapeDtypeStruct((rows, 512), bf16),
+            pltpu.VMEM((rows, 512), bf16),
             jax.ShapeDtypeStruct((rows * peers, 256), bf16),
         ),
         in_specs=[vmem] * 3 + [hbm] * 4,
@@ -731,7 +731,9 @@
     queries, kv = gather_and_project(
         node_rows, node_target, node_position, w_query, w_key, w_value
     )
+    queries = pltpu.with_memory_space_constraint(queries, pltpu.VMEM)
     attended = attend(block_mask, queries, kv)
+    attended = pltpu.with_memory_space_constraint(attended, pltpu.VMEM)
     return project_out(attended, w_out)
 
 

time: 123 us -> 117 us (0.951)
  Pallas kernels: 120 us -> 117 us
    pallas_call x3, Pallas kernels: 120 us -> 117 us  [the longest x1 69.7 us: gather_and_project(): pl.pallas_call(gather_kernel, out_shape=(pltpu.VMEM((rows, 512), bf16), j...]
where the time goes in v8:
time: 117 us
  Pallas kernels  117 us (100%)
    pallas_call x1, Pallas kernels, gather_and_project(): pl.pallas_call(gather_kernel, out_shape=(pltpu.VMEM((rows, 512), bf16), j...  69.7 us
    pallas_call x1, Pallas kernels, project_out(): pl.pallas_call(project_out_kernel, out_shape=pltpu.VMEM((seat, width), bf...  39.3 us
    pallas_call x1, Pallas kernels, attend(): pl.pallas_call(attend_kernel, out_shape=pltpu.VMEM(queries.shape, jnp.bfl...  7.43 us

profile of v8, /device:TPU:34, one launch (start us, length us, event | category | flops | bytes accessed | tf_op | source)
XLA Modules:
  0.0 117.3 jit_solution(5462473249771881317)
XLA Ops:
  0.0 69.7 %gather_and_project.1 = (bf16[512,512]{1,0:T(8,128)(2,1)S(1)}, bf16[8192,256]{1,0:T(8,128)(2,1)}) custom-call(s32[1,512]{1,0:T(1,128)} %bitcast.2, s32[1,512]{1,0:T(1,128)} %bitcast.3, f32[2,128]{1,0:T(2,128)} %constant.2.clone.turn_ref, bf16[512,512]{1,0:T(8,128)(2,1)} %x_hbm.1, bf16[4096,512]{1,0:T(8,128)(2,1)} %wq_hbm.1, bf16[4096,128]{1,0:T(8,128)(2,1)} %wk_hbm.1, ...), custom_call_target="tpu_custom_call" | custom-call | tf_op jit(solution)/shard_map/gather_and_project/pallas_call | solution.py:687
  69.7 7.4 %attend.1.att_ref = bf16[512,512]{1,0:T(8,128)(2,1)S(1)} custom-call(s32[4,64]{1,0:T(4,128)} %mask_ref.1, bf16[512,512]{1,0:T(8,128)(2,1)S(1)} %get-tuple-element.7.q_ref, bf16[8192,256]{1,0:T(8,128)(2,1)} %get-tuple-element.8.kv_hbm), custom_call_target="tpu_custom_call" | custom-call | tf_op jit(solution)/shard_map/attend/pallas_call | solution.py:109
  77.2 39.3 %project_out.1 = bf16[64,4096]{1,0:T(8,128)(2,1)S(1)} custom-call(bf16[512,512]{1,0:T(8,128)(2,1)S(1)} %attend.1.att_ref, bf16[512,4096]{1,0:T(8,128)(2,1)} %w_hbm.1), custom_call_target="tpu_custom_call" | custom-call | tf_op jit(solution)/shard_map/project_out/pallas_call | solution.py:292
  116.5 0.8 copy.11

commit v9 on v8

--- a/solution.py
+++ b/solution.py
@@ -148,7 +148,7 @@
     )
 
 
-OUT_CHUNKS = 8
+OUT_CHUNKS = 4
 
 
 def project_out_kernel(

time: 117 us -> 117 us (level)
    pallas_call x1, Pallas kernels: 39.3 us -> 38 us  [project_out(): pl.pallas_call(project_out_kernel, out_shape=pltpu.VMEM((seat, width), bf...]
where the time goes in v9:
time: 117 us
  Pallas kernels  116 us (99%)
    pallas_call x1, Pallas kernels, gather_and_project(): pl.pallas_call(gather_kernel, out_shape=(pltpu.VMEM((rows, 512), bf16), j...  69.7 us
    pallas_call x1, Pallas kernels, project_out(): pl.pallas_call(project_out_kernel, out_shape=pltpu.VMEM((seat, width), bf...  38 us
    pallas_call x1, Pallas kernels, attend(): pl.pallas_call(attend_kernel, out_shape=pltpu.VMEM(queries.shape, jnp.bfl...  8.24 us

profile of v9, /device:TPU:34, one launch (start us, length us, event | category | flops | bytes accessed | tf_op | source)
XLA Modules:
  0.0 116.8 jit_solution(9474460498995331469)
XLA Ops:
  0.0 69.7 %gather_and_project.1 = (bf16[512,512]{1,0:T(8,128)(2,1)S(1)}, bf16[8192,256]{1,0:T(8,128)(2,1)}) custom-call(s32[1,512]{1,0:T(1,128)} %bitcast.2, s32[1,512]{1,0:T(1,128)} %bitcast.3, f32[2,128]{1,0:T(2,128)} %constant.2.clone.turn_ref, bf16[512,512]{1,0:T(8,128)(2,1)} %x_hbm.1, bf16[4096,512]{1,0:T(8,128)(2,1)} %wq_hbm.1, bf16[4096,128]{1,0:T(8,128)(2,1)} %wk_hbm.1, ...), custom_call_target="tpu_custom_call" | custom-call | tf_op jit(solution)/shard_map/gather_and_project/pallas_call | solution.py:687
  69.7 8.2 %attend.1.att_ref = bf16[512,512]{1,0:T(8,128)(2,1)S(1)} custom-call(s32[4,64]{1,0:T(4,128)} %mask_ref.1, bf16[512,512]{1,0:T(8,128)(2,1)S(1)} %get-tuple-element.7.q_ref, bf16[8192,256]{1,0:T(8,128)(2,1)} %get-tuple-element.8.kv_hbm), custom_call_target="tpu_custom_call" | custom-call | tf_op jit(solution)/shard_map/attend/pallas_call | solution.py:109
  78.0 38.0 %project_out.1 = bf16[64,4096]{1,0:T(8,128)(2,1)S(1)} custom-call(bf16[512,512]{1,0:T(8,128)(2,1)S(1)} %attend.1.att_ref, bf16[512,4096]{1,0:T(8,128)(2,1)} %w_hbm.1), custom_call_target="tpu_custom_call" | custom-call | tf_op jit(solution)/shard_map/project_out/pallas_call | solution.py:292
  116.0 0.8 copy.11
